TPU v7x, 128 devices: a whole 4x4x4 slice. The times are simulated.
128 devices in a mesh: dom: 128 (over y, x, z, core).
Axes of the slice: x: 4, y: 4, z: 4, core: 2. Of those that a mesh axis runs over, the one named last changes fastest.
Arguments:
- initial_dofs: float32 [4, 35, 32768], P(None, None, 'dom'), may hold values from -6 to 6
- cluster: int32 [32768], P('dom'), may hold values from 0 to 2, as said below
- neighbours: int32 [4, 32768], P(None, 'dom'), may hold values from -2 to 255, as said below
- orientation: int32 [4, 32768], P(None, 'dom'), may hold values from 0 to 23, as said below
- send_slots: int32 [8, 8192], P(None, 'dom'), may hold values from -1 to 1023, as said below
- recv_slots: int32 [8, 8192], P(None, 'dom'), may hold values from -1 to 1023, as said below
- inv_jacobian: float32 [3, 3, 32768], P(None, None, 'dom'), may hold values from -3 to 3
- normals: float32 [4, 3, 32768], P(None, None, 'dom'), may hold values from -1 to 1, as said below
- face_area: float32 [4, 32768], P(None, 'dom'), may hold values from 0.3 to 1
- bulk_modulus: float32 [32768], P('dom'), may hold values from 0.5 to 2
- inv_density: float32 [32768], P('dom'), may hold values from 0.5 to 2
- deriv_mats: float32 [3, 35, 35], replicated, may hold values from -1 to 1
- face_proj: float32 [4, 15, 35], replicated, may hold values from -1 to 1
Outputs:
- final_dofs: float32 [4, 35, 32768], P(None, None, 'dom')
Inputs may be any that keep to these rules, and one draw needn't show every extreme that they name: Within each partition the cluster numbers never fall along the element numbers; each of 0, 1 and 2 holds a positive multiple of 32 elements of every partition. `neighbours`: local element numbers within the same partition, -1 for a wall face, and -2 exactly for the faces listed in recv_slots (which are also exactly those listed in send_slots) of the same partition. For a face listed in recv_slots, orientation // 6 is the face number (0 to 3) of the sending face. `send_slots`: face numbers f * 256 + e of the partition, -1 for empty slots; the live slots of each row come first; the count of live slots in row k of partition r equals that in row 7 - k of partition r + offset_k, zero where that partition does not exist; no face appears twice in a partition; rows of offset 1 and -1 are full wherever the partner exists. `recv_slots`: same encoding and counts as send_slots of the same partition and row, the same set of faces in another order; slot j of row k takes what slot j of row 7 - k of partition r + offset_k sends. `normals`: unit vectors.
All inputs are finite; a program needn't handle non-finite values.
Results may differ from a plain program's by a relative error of at most 0.0003.
Values sent between devices are 32-bit elements; how exact they have to be, the bound alone decides.
A program may use at most 128 MiB of HBM per device.

v0:
```python
import math

import jax
import jax.numpy as jnp
import numpy as np
from jax import lax
from jax.sharding import PartitionSpec as P

SUBSTEPS = 4


STEP_LENGTH = 0.3
HIGH = lax.Precision.HIGHEST
LANE_WIDTH = 128


def passed_along(value, axis, steps):
    count = lax.axis_size(axis)
    leading, last = (max(0, -steps), min(count, count - steps))
    return lax.ppermute(value, axis, [(source, source + steps) for source in range(leading, last)])


def node_orders():
    node_list = [(i, j) for i in range(5) for j in range(5 - i)]
    place_of = {lattice_node: position for position, lattice_node in enumerate(node_list)}
    turn_list = [(0, 1, 2), (1, 2, 0), (2, 0, 1), (0, 2, 1), (2, 1, 0), (1, 0, 2)]
    order_table = []
    for one_turn in turn_list:
        row_list = []
        for lattice_node in node_list:
            corner_triple = (
                lattice_node[0],
                lattice_node[1],
                4 - lattice_node[0] - lattice_node[1],
            )
            row_list.append(place_of[corner_triple[one_turn[0]], corner_triple[one_turn[1]]])
        order_table.append(row_list)
    return np.array(order_table, dtype=np.int32)


def element_periods(cluster):
    return jnp.where(cluster == 0, 1, jnp.where(cluster == 1, 2, 4)).astype(jnp.int32)


def block_width(elem_count):
    return LANE_WIDTH if elem_count % LANE_WIDTH == 0 else elem_count


def derivative_rows(values, deriv_mats, inv_jacobian):
    mixed = jnp.einsum("jab,qbe->jqae", deriv_mats, values, precision=HIGH)
    divergence = jnp.einsum("jie,jiae->ae", inv_jacobian, mixed[:, 1:], precision=HIGH)
    gradient = jnp.einsum("jie,jae->iae", inv_jacobian, mixed[:, 0], precision=HIGH)
    return (divergence, gradient)


def spatial(values, deriv_mats, inv_jacobian, bulk_modulus, inv_density):
    divergence, gradient = derivative_rows(values, deriv_mats, inv_jacobian)
    return jnp.concatenate([(-bulk_modulus * divergence)[None], -inv_density * gradient], axis=0)


def volume_term(values, deriv_mats, inv_jacobian, bulk_modulus, inv_density):
    divergence, gradient = derivative_rows(values, jnp.swapaxes(deriv_mats, 1, 2), inv_jacobian)
    return jnp.concatenate([(bulk_modulus * divergence)[None], inv_density * gradient], axis=0)


def predict(s, values, taylor, cluster, deriv_mats, inv_jacobian, bulk_modulus, inv_density):
    elem_count = values.shape[2]
    block_size = block_width(elem_count)
    pieces = []
    for block_index in range(elem_count // block_size):
        lower = block_index * block_size
        upper = lower + block_size
        start_mask = s % element_periods(cluster[lower:upper]) == 0
        kept = tuple((term[:, :, lower:upper] for term in taylor))

        def fresh_terms(operands):
            vals_now, jac_now, bulk_now, density_now, kept_now, mask_now = operands
            terms = [vals_now]
            for term_index in range(1, 5):
                terms.append(spatial(terms[-1], deriv_mats, jac_now, bulk_now, density_now))
            return tuple((jnp.where(mask_now, terms[i], kept_now[i]) for i in range(5)))

        def kept_terms(operands):
            return operands[4]

        pieces.append(
            lax.cond(
                jnp.any(start_mask),
                fresh_terms,
                kept_terms,
                (
                    values[:, :, lower:upper],
                    inv_jacobian[:, :, lower:upper],
                    bulk_modulus[lower:upper],
                    inv_density[lower:upper],
                    kept,
                    start_mask,
                ),
            )
        )
    taylor = tuple(
        (
            jnp.concatenate([piece[term_index] for piece in pieces], axis=2)
            for term_index in range(5)
        )
    )
    phase = s % element_periods(cluster)
    begin = phase.astype(jnp.float32) * STEP_LENGTH
    finish = begin + STEP_LENGTH
    integral = jnp.zeros_like(values)
    for term_index in range(5):
        weight_now = (finish ** (term_index + 1) - begin ** (term_index + 1)) / math.factorial(
            term_index + 1
        )
        integral = integral + taylor[term_index] * weight_now
    return (taylor, integral)


def face_traces(values, face_proj):
    traced = jnp.einsum("fnb,qbe->qnfe", face_proj, values, precision=HIGH)
    return traced.reshape(traced.shape[0], traced.shape[1], -1)


def rotate_faces(raw_traces, codes):
    order_table = node_orders()
    turn_code = codes % 6
    result = jnp.zeros_like(raw_traces)
    for turn_index in range(6):
        result = result + jnp.where(
            turn_code == turn_index, raw_traces[:, order_table[turn_index], :], 0.0
        )
    return result


def apply_update(
    s,
    values,
    integral_sum,
    neighbour_sum,
    cluster,
    neighbours,
    orientation,
    normals,
    face_area,
    bulk_modulus,
    inv_density,
    deriv_mats,
    inv_jacobian,
    face_proj,
):
    finished = (s + 1) % element_periods(cluster) == 0
    own_side = jnp.einsum("fnb,qbe->qnfe", face_proj, integral_sum, precision=HIGH)
    far_side = rotate_faces(neighbour_sum, orientation.reshape(-1)).reshape(own_side.shape)
    wall = (neighbours == -1)[None]
    direction = jnp.swapaxes(normals, 0, 1)[:, None]
    normal_own = jnp.sum(direction * own_side[1:], axis=0)
    normal_far = jnp.where(wall, -normal_own, jnp.sum(direction * far_side[1:], axis=0))
    pressure_own = own_side[0]
    pressure_far = jnp.where(wall, pressure_own, far_side[0])
    impedance = jnp.sqrt(bulk_modulus / inv_density)
    pressure_star = 0.5 * (pressure_own + pressure_far) + 0.5 * impedance * (
        normal_own - normal_far
    )
    velocity_star = (
        0.5 * (normal_own + normal_far) + 0.5 * (pressure_own - pressure_far) / impedance
    )
    flux_pressure = bulk_modulus * velocity_star * face_area
    flux_velocity = direction * (inv_density * pressure_star * face_area)[None]
    flux = jnp.concatenate([flux_pressure[None], flux_velocity], axis=0)
    lifted = jnp.einsum("fnb,qnfe->qbe", face_proj, flux, precision=HIGH)
    change = volume_term(integral_sum, deriv_mats, inv_jacobian, bulk_modulus, inv_density) - lifted
    values = jnp.where(finished, values + change, values)
    integral_sum = jnp.where(finished, 0.0, integral_sum)
    neighbour_sum = jnp.where(jnp.tile(finished, 4), 0.0, neighbour_sum)
    return (values, integral_sum, neighbour_sum)


def update_blocks(
    s,
    values,
    integral_sum,
    neighbour_sum,
    cluster,
    neighbours,
    orientation,
    normals,
    face_area,
    bulk_modulus,
    inv_density,
    deriv_mats,
    inv_jacobian,
    face_proj,
):
    elem_count = values.shape[2]
    block_size = block_width(elem_count)
    near_faces = neighbour_sum.reshape(
        neighbour_sum.shape[0], neighbour_sum.shape[1], 4, elem_count
    )
    value_parts, own_parts, near_parts = ([], [], [])
    for block_index in range(elem_count // block_size):
        lower = block_index * block_size
        upper = lower + block_size
        finished_any = jnp.any((s + 1) % element_periods(cluster[lower:upper]) == 0)
        operands = (
            values[:, :, lower:upper],
            integral_sum[:, :, lower:upper],
            near_faces[:, :, :, lower:upper].reshape(near_faces.shape[0], near_faces.shape[1], -1),
            cluster[lower:upper],
            neighbours[:, lower:upper],
            orientation[:, lower:upper],
            normals[:, :, lower:upper],
            face_area[:, lower:upper],
            bulk_modulus[lower:upper],
            inv_density[lower:upper],
            inv_jacobian[:, :, lower:upper],
        )

        def updated(items):
            return apply_update(
                s,
                items[0],
                items[1],
                items[2],
                items[3],
                items[4],
                items[5],
                items[6],
                items[7],
                items[8],
                items[9],
                deriv_mats,
                items[10],
                face_proj,
            )

        def unchanged(items):
            return (items[0], items[1], items[2])

        vals_now, own_now, near_now = lax.cond(finished_any, updated, unchanged, operands)
        value_parts.append(vals_now)
        own_parts.append(own_now)
        near_parts.append(near_now.reshape(near_now.shape[0], near_now.shape[1], 4, block_size))
    values = jnp.concatenate(value_parts, axis=2)
    integral_sum = jnp.concatenate(own_parts, axis=2)
    neighbour_sum = jnp.concatenate(near_parts, axis=3).reshape(neighbour_sum.shape)
    return (values, integral_sum, neighbour_sum)


def body(
    initial_dofs,
    cluster,
    neighbours,
    orientation,
    send_slots,
    recv_slots,
    inv_jacobian,
    normals,
    face_area,
    bulk_modulus,
    inv_density,
    deriv_mats,
    face_proj,
):
    offset_count, slot_count = send_slots.shape
    reach_now = offset_count // 2
    offsets = [k - reach_now if k < reach_now else k - reach_now + 1 for k in range(offset_count)]
    elem_count = initial_dofs.shape[2]
    face_total = 4 * elem_count
    values = initial_dofs
    taylor = tuple((jnp.zeros_like(values) for term_index in range(5)))
    integral_sum = jnp.zeros_like(values)
    neighbour_sum = jnp.zeros((values.shape[0], face_proj.shape[1], face_total), jnp.float32)
    send_live = (send_slots >= 0).reshape(-1)
    send_index = jnp.maximum(send_slots, 0).reshape(-1)
    sender_face = orientation.reshape(-1)[jnp.maximum(recv_slots, 0)] // 6
    flat_nbr = neighbours.reshape(-1)
    local_live = flat_nbr >= 0
    local_source = orientation.reshape(-1) // 6 * elem_count + jnp.maximum(flat_nbr, 0)
    recv_flat = recv_slots.reshape(-1)
    slot_of_face = (
        jnp.full((face_total,), -1, jnp.int32)
        .at[jnp.where(recv_flat >= 0, recv_flat, face_total)]
        .set(jnp.arange(recv_flat.shape[0], dtype=jnp.int32), mode="drop")
    )
    remote_live = slot_of_face >= 0
    remote_source = jnp.maximum(slot_of_face, 0)
    for s in range(SUBSTEPS):
        taylor, integral = predict(
            s, values, taylor, cluster, deriv_mats, inv_jacobian, bulk_modulus, inv_density
        )
        integral_sum = integral_sum + integral
        traced = face_traces(integral, face_proj)
        local_part = jnp.where(local_live, traced[:, :, local_source], 0.0)
        outgoing = integral[:, :, send_index % elem_count]
        outgoing = jnp.where(send_live, outgoing, 0.0).reshape(
            outgoing.shape[0], outgoing.shape[1], offset_count, slot_count
        )
        arrived = [None] * offset_count
        for k in range(offset_count):
            arrived[offset_count - 1 - k] = passed_along(outgoing[:, :, k], "dom", offsets[k])
        received = jnp.stack(arrived, axis=2)
        projected = jnp.einsum("fnb,qbkc->fqnkc", face_proj, received, precision=HIGH)
        chosen = jnp.zeros(projected.shape[1:], jnp.float32)
        for face_index in range(4):
            chosen = chosen + jnp.where(sender_face == face_index, projected[face_index], 0.0)
        received = chosen
        received_flat = received.reshape(received.shape[0], received.shape[1], -1)
        raw_traces = jnp.where(remote_live, received_flat[:, :, remote_source], local_part)
        neighbour_sum = neighbour_sum + raw_traces
        values, integral_sum, neighbour_sum = update_blocks(
            s,
            values,
            integral_sum,
            neighbour_sum,
            cluster,
            neighbours,
            orientation,
            normals,
            face_area,
            bulk_modulus,
            inv_density,
            deriv_mats,
            inv_jacobian,
            face_proj,
        )
    return values


def solution(mesh):
    return jax.shard_map(
        body,
        mesh=mesh,
        in_specs=(
            P(None, None, "dom"),
            P("dom"),
            P(None, "dom"),
            P(None, "dom"),
            P(None, "dom"),
            P(None, "dom"),
            P(None, None, "dom"),
            P(None, None, "dom"),
            P(None, "dom"),
            P("dom"),
            P("dom"),
            P(),
            P(),
        ),
        out_specs=P(None, None, "dom"),
        check_vma=False,
    )
```

profile of v0, /device:TPU:25, one launch (start us, length us, event | category | flops | bytes accessed | tf_op | source)
XLA Modules:
  0.0 1101.3 jit_solution(13291494746393681961)
XLA Ops:
  8.3 24.8 %conditional.17 = (f32[4,35,128]{1,0,2:T(4,128)S(1)}, f32[4,35,128]{1,0,2:T(4,128)S(1)}, f32[4,35,128]{1,0,2:T(4,128)S(1)}, f32[4,35,128]{1,0,2:T(4,128)S(1)}, f32[4,35,128]{1,0,2:T(4,128)S(1)}) conditional(s32[]{:T(128)} %convert_element_type.53, () %tuple.193, (pred[128]{0:T(512)(128)(4,1)S(1)}, f32[4,35,128]{1,0,2:T(4,128)S(1)}, f32[128]{0:T(128)}, ...), branch_computations={%region_8.9_spmd, %region_9.10_spmd} | conditional | flops 94420736 | bytes 6970788 | solution.py:87
  36.4 38.2 %conditional.16 = (f32[4,35,128]{1,0,2:T(4,128)S(1)}, f32[4,35,128]{1,0,2:T(4,128)S(1)}, f32[4,35,128]{1,0,2:T(4,128)S(1)}, f32[4,35,128]{1,0,2:T(4,128)}, f32[4,35,128]{1,0,2:T(4,128)S(1)}) conditional(s32[]{:T(128)} %convert_element_type.52, () %tuple.191, (pred[128]{0:T(512)(128)(4,1)S(1)}, f32[4,35,128]{1,0,2:T(4,128)S(1)}, f32[128]{0:T(128)S(1)}, ...), branch_computations={%region_5.6_spmd, %region_6.7_spmd} | conditional | flops 94420736 | bytes 8691164 | solution.py:87
  127.7 9.5 gather_fusion.51
  142.3 6.2 collective-permute-start.5
  174.0 7.3 fusion.461
  181.3 9.2 gather_fusion.50
  198.8 48.9 %conditional.19 = (f32[4,35,128]{1,0,2:T(4,128)S(1)}, f32[4,15,4,128]{3,2,0,1:T(4,128)}, f32[4,35,128]{2,0,1:T(4,128)}) conditional(s32[]{:T(128)} %convert_element_type.55, (f32[4,35,128]{1,0,2:T(4,128)S(1)}, f32[4,35,128]{2,0,1:T(4,128)}, f32[4,15,512]{2,0,1:T(4,128)}) %tuple.197, (s32[128]{0:T(128)}, f32[128]{0:T(128)}, ...), branch_computations={%region_16.17_spmd, %region_17.20_spmd} | conditional | flops 50111540 | bytes 8211942 | solution.py:239
  247.7 60.3 %conditional.21 = ((f32[4,35,128]{1,0,2:T(4,128)S(1)}, f32[4,35,128]{1,0,2:T(4,128)S(1)}, f32[4,35,128]{1,0,2:T(4,128)S(1)}, f32[4,35,128]{1,0,2:T(4,128)S(1)}, f32[4,35,128]{1,0,2:T(4,128)S(1)})) conditional(s32[]{:T(128)} %convert_element_type.55, (f32[4,35,128]{1,0,2:T(4,128)S(1)}, f32[4,35,128]{1,0,2:T(4,128)S(1)}, ...), branch_computations={%region_22.23_spmd, %region_23.24_spmd} | conditional | flops 94420736 | bytes 10713736 | solution.py:87
  308.8 47.7 %conditional.18 = (f32[4,35,128]{1,0,2:T(4,128)S(1)}, f32[4,15,4,128]{3,2,0,1:T(4,128)}, f32[4,35,128]{2,0,1:T(4,128)}) conditional(s32[]{:T(128)} %convert_element_type.51, (f32[4,35,128]{1,0,2:T(4,128)S(1)}, f32[4,35,128]{2,0,1:T(4,128)}, f32[4,15,512]{2,0,1:T(4,128)}) %tuple.195, (s32[128]{0:T(128)}, f32[128]{0:T(128)}, ...), branch_computations={%region_11.12_spmd, %region_12.15_spmd} | conditional | flops 50111540 | bytes 8214018 | solution.py:239
  356.5 59.9 %conditional.20 = ((f32[4,35,128]{1,0,2:T(4,128)S(1)}, f32[4,35,128]{1,0,2:T(4,128)S(1)}, f32[4,35,128]{1,0,2:T(4,128)S(1)}, f32[4,35,128]{1,0,2:T(4,128)}, f32[4,35,128]{1,0,2:T(4,128)S(1)})) conditional(s32[]{:T(128)} %convert_element_type.51, (f32[4,35,128]{1,0,2:T(4,128)S(1)}, f32[4,35,128]{1,0,2:T(4,128)S(1)}, f32[4,35,128]{1,0,2:T(4,128)S(1)}, ...), branch_computations={%region_20.21_spmd, %region_21.22_spmd} | conditional | flops 94420736 | bytes 10713736 | solution.py:87
  453.8 9.5 gather_fusion.54
  465.9 7.2 collective-permute-start.13
  499.9 7.3 fusion.458
  507.2 9.2 gather_fusion.53
  524.3 48.6 %conditional.23 = (f32[4,35,128]{1,0,2:T(4,128)S(1)}, f32[4,15,4,128]{3,2,0,1:T(4,128)}, f32[4,35,128]{2,0,1:T(4,128)}) conditional(s32[]{:T(128)} %convert_element_type.57, (f32[4,35,128]{1,0,2:T(4,128)S(1)}, f32[4,35,128]{2,0,1:T(4,128)}, f32[4,15,512]{2,0,1:T(4,128)}) %tuple.203, (s32[128]{0:T(128)}, f32[128]{0:T(128)}, ...), branch_computations={%region_29.30_spmd, %region_30.33_spmd} | conditional | flops 50111540 | bytes 8211942 | solution.py:239
  572.9 60.6 %conditional.25 = ((f32[4,35,128]{1,0,2:T(4,128)S(1)}, f32[4,35,128]{1,0,2:T(4,128)S(1)}, f32[4,35,128]{1,0,2:T(4,128)S(1)}, f32[4,35,128]{1,0,2:T(4,128)S(1)}, f32[4,35,128]{1,0,2:T(4,128)S(1)})) conditional(s32[]{:T(128)} %convert_element_type.57, (f32[4,35,128]{1,0,2:T(4,128)S(1)}, f32[4,35,128]{1,0,2:T(4,128)S(1)}, ...), branch_computations={%region_35.36_spmd, %region_36.37_spmd} | conditional | flops 94420736 | bytes 10713736 | solution.py:87
  634.3 47.8 %conditional.22 = (f32[4,35,128]{1,0,2:T(4,128)S(1)}, f32[4,15,4,128]{3,2,0,1:T(4,128)}, f32[4,35,128]{2,0,1:T(4,128)}) conditional(s32[]{:T(128)} %convert_element_type.50, (f32[4,35,128]{1,0,2:T(4,128)S(1)}, f32[4,35,128]{2,0,1:T(4,128)}, f32[4,15,512]{2,0,1:T(4,128)}) %tuple.201, (s32[128]{0:T(128)}, f32[128]{0:T(128)}, ...), branch_computations={%region_24.25_spmd, %region_25.28_spmd} | conditional | flops 50111540 | bytes 8214018 | solution.py:239
  682.1 59.9 %conditional.24 = ((f32[4,35,128]{1,0,2:T(4,128)S(1)}, f32[4,35,128]{1,0,2:T(4,128)S(1)}, f32[4,35,128]{1,0,2:T(4,128)S(1)}, f32[4,35,128]{1,0,2:T(4,128)}, f32[4,35,128]{1,0,2:T(4,128)S(1)})) conditional(s32[]{:T(128)} %convert_element_type.50, (f32[4,35,128]{1,0,2:T(4,128)S(1)}, f32[4,35,128]{1,0,2:T(4,128)S(1)}, f32[4,35,128]{1,0,2:T(4,128)S(1)}, ...), branch_computations={%region_33.34_spmd, %region_34.35_spmd} | conditional | flops 94420736 | bytes 10713736 | solution.py:87
  777.5 9.5 gather_fusion.57
  789.6 7.7 collective-permute-start.21
  804.1 5.5 collective-permute-start.23
  823.9 7.3 fusion.455
  831.2 9.2 gather_fusion.56
  848.3 48.6 %conditional.27 = (f32[4,35,128]{1,0,2:T(4,128)S(1)}, f32[4,15,4,128]{3,2,0,1:T(4,128)}, f32[4,35,128]{2,0,1:T(4,128)}) conditional(s32[]{:T(128)} %convert_element_type.59, (f32[4,35,128]{1,0,2:T(4,128)S(1)}, f32[4,35,128]{2,0,1:T(4,128)}, f32[4,15,512]{2,0,1:T(4,128)}) %tuple.209, (s32[128]{0:T(128)}, f32[128]{0:T(128)}, ...), branch_computations={%region_42.43_spmd, %region_43.46_spmd} | conditional | flops 50111540 | bytes 8211942 | solution.py:239
  897.6 50.7 %conditional.29 = (f32[4,35,128]{2,0,1:T(4,128)}, f32[4,35,128]{2,0,1:T(4,128)S(1)}, f32[4,35,128]{2,0,1:T(4,128)S(1)}, f32[4,35,128]{2,0,1:T(4,128)}, f32[4,35,128]{2,0,1:T(4,128)S(1)}) conditional(s32[]{:T(128)} %convert_element_type.59, (f32[4,35,128]{1,0,2:T(4,128)S(1)}, f32[4,35,128]{1,0,2:T(4,128)S(1)}, f32[4,35,128]{1,0,2:T(4,128)S(1)}, ...), branch_computations={%region_48.49_spmd, %region_49.50_spmd} | conditional | flops 94420736 | bytes 10291952 | solution.py:87
  949.1 25.6 %conditional.26 = (f32[4,35,128]{1,0,2:T(4,128)S(1)}, f32[4,15,4,128]{3,2,0,1:T(4,128)S(1)}, f32[4,35,128]{2,0,1:T(4,128)}) conditional(s32[]{:T(128)} %convert_element_type.49, (f32[4,35,128]{1,0,2:T(4,128)S(1)}, f32[4,35,128]{2,0,1:T(4,128)}, f32[4,15,512]{2,0,1:T(4,128)}) %tuple.207, (s32[128]{0:T(128)}, f32[128]{0:T(128)S(1)}, ...), branch_computations={%region_37.38_spmd, %region_38.41_spmd} | conditional | flops 50111540 | bytes 8498690 | solution.py:239
  975.4 24.3 %conditional.28 = (f32[4,35,128]{2,0,1:T(4,128)}, f32[4,35,128]{2,0,1:T(4,128)}, f32[4,35,128]{2,0,1:T(4,128)}, f32[4,35,128]{2,0,1:T(4,128)}, f32[4,35,128]{2,0,1:T(4,128)}) conditional(s32[]{:T(128)} %convert_element_type.49, (f32[4,35,128]{1,0,2:T(4,128)S(1)}, f32[4,35,128]{1,0,2:T(4,128)S(1)}, f32[4,35,128]{1,0,2:T(4,128)S(1)}, ...), branch_computations={%region_46.47_spmd, %region_47.48_spmd} | conditional | flops 94420736 | bytes 7987160 | solution.py:87
  1019.2 8.0 gather_fusion.60
  1029.7 7.6 collective-permute-start.29
  1060.1 6.9 fusion.452
  1074.7 13.4 %conditional.31 = (f32[4,35,128]{2,0,1:T(4,128)S(1)}) conditional(s32[]{:T(128)} %convert_element_type.61, f32[4,35,128]{1,0,2:T(4,128)S(1)} %get-tuple-element.1141, (s32[128]{0:T(128)}, f32[128]{0:T(128)}, f32[4,35,256]{2,0,1:T(4,128)S(1)}, f32[3,35,35]{2,1,0:T(8,128)S(1)}, f32[3,3,128]{0,1,2:T(4,128)S(1)}, /*index=5*/f32[128]{0:T(128)}, ...), branch_computations={%region_55.56_spmd, %region_56.59_spmd} | conditional | flops 50062900 | bytes 6458566 | solution.py:239
  1088.7 10.5 conditional.30
  (1293 shorter events, 953.1 us)
Async XLA Ops:
  95.4 46.9 %collective-permute-start = (f32[4,35,64]{2,1,0:T(8,128)}, f32[4,35,64]{2,1,0:T(8,128)}, u32[]{:S(2)}, u32[]{:S(2)}) collective-permute-start(f32[4,35,64]{2,1,0:T(8,128)} %get-tuple-element.3094), channel_id=1, source_target_pairs={{0,4},{1,5},{2,6},{3,7},{4,8},{5,9},{6,10},{7,11},{8,12},{9,13},{1... | collective-permute-start | bytes 107528 | tf_op jit(solution)/shard_map/ppermute | solution.py:20
  100.9 48.5 %collective-permute-start.1 = (f32[4,35,64]{2,1,0:T(8,128)}, f32[4,35,64]{2,1,0:T(8,128)}, u32[]{:S(2)}, u32[]{:S(2)}) collective-permute-start(f32[4,35,64]{2,1,0:T(8,128)} %get-tuple-element.3093), channel_id=1, source_target_pairs={{0,3},{1,4},{2,5},{3,6},{4,7},{5,8},{6,9},{7,10},{8,11},{9,12},{10... | collective-permute-start | bytes 107528 | tf_op jit(solution)/shard_map/ppermute | solution.py:20
  104.0 50.5 %collective-permute-start.2 = (f32[4,35,64]{2,1,0:T(8,128)}, f32[4,35,64]{2,1,0:T(8,128)}, u32[]{:S(2)}, u32[]{:S(2)}) collective-permute-start(f32[4,35,64]{2,1,0:T(8,128)} %get-tuple-element.3092), channel_id=1, source_target_pairs={{0,2},{1,3},{2,4},{3,5},{4,6},{5,7},{6,8},{7,9},{8,10},{9,11},{10,... | collective-permute-start | bytes 107528 | tf_op jit(solution)/shard_map/ppermute | solution.py:20
  107.5 51.6 %collective-permute-start.3 = (f32[4,35,64]{2,1,0:T(8,128)}, f32[4,35,64]{2,1,0:T(8,128)}, u32[]{:S(2)}, u32[]{:S(2)}) collective-permute-start(f32[4,35,64]{2,1,0:T(8,128)} %get-tuple-element.3091), channel_id=1, source_target_pairs={{0,1},{1,2},{2,3},{3,4},{4,5},{5,6},{6,7},{7,8},{8,9},{9,10},{10,1... | collective-permute-start | bytes 107528 | tf_op jit(solution)/shard_map/ppermute | solution.py:20
  109.5 50.6 %collective-permute-start.4 = (f32[4,35,64]{2,1,0:T(8,128)}, f32[4,35,64]{2,1,0:T(8,128)}, u32[]{:S(2)}, u32[]{:S(2)}) collective-permute-start(f32[4,35,64]{2,1,0:T(8,128)} %get-tuple-element.3090), channel_id=1, source_target_pairs={{1,0},{2,1},{3,2},{4,3},{5,4},{6,5},{7,6},{8,7},{9,8},{10,9},{11,1... | collective-permute-start | bytes 107528 | tf_op jit(solution)/shard_map/ppermute | solution.py:20
  142.3 18.6 %collective-permute-start.5 = (f32[4,35,64]{2,1,0:T(8,128)}, f32[4,35,64]{2,1,0:T(8,128)S(1)}, u32[]{:S(2)}, u32[]{:S(2)}) collective-permute-start(f32[4,35,64]{2,1,0:T(8,128)} %get-tuple-element.3089), channel_id=1, source_target_pairs={{2,0},{3,1},{4,2},{5,3},{6,4},{7,5},{8,6},{9,7},{10,8},{11,9},{12,... | collective-permute-start | bytes 107528 | tf_op jit(solution)/shard_map/ppermute | solution.py:20
  149.4 11.5 %collective-permute-start.6 = (f32[4,35,64]{2,1,0:T(8,128)}, f32[4,35,64]{2,1,0:T(8,128)S(1)}, u32[]{:S(2)}, u32[]{:S(2)}) collective-permute-start(f32[4,35,64]{2,1,0:T(8,128)} %get-tuple-element.3088), channel_id=1, source_target_pairs={{3,0},{4,1},{5,2},{6,3},{7,4},{8,5},{9,6},{10,7},{11,8},{12,9},{13... | collective-permute-start | bytes 107528 | tf_op jit(solution)/shard_map/ppermute | solution.py:20
  154.4 8.1 collective-permute-start.7
  437.0 28.9 %collective-permute-start.8 = (f32[4,35,64]{2,1,0:T(8,128)}, f32[4,35,64]{2,1,0:T(8,128)}, u32[]{:S(2)}, u32[]{:S(2)}) collective-permute-start(f32[4,35,64]{2,1,0:T(8,128)} %get-tuple-element.3086), channel_id=1, source_target_pairs={{0,4},{1,5},{2,6},{3,7},{4,8},{5,9},{6,10},{7,11},{8,12},{9,13},{1... | collective-permute-start | bytes 107528 | tf_op jit(solution)/shard_map/ppermute | solution.py:20
  441.4 32.5 %collective-permute-start.9 = (f32[4,35,64]{2,1,0:T(8,128)}, f32[4,35,64]{2,1,0:T(8,128)}, u32[]{:S(2)}, u32[]{:S(2)}) collective-permute-start(f32[4,35,64]{2,1,0:T(8,128)} %get-tuple-element.3085), channel_id=1, source_target_pairs={{0,3},{1,4},{2,5},{3,6},{4,7},{5,8},{6,9},{7,10},{8,11},{9,12},{10... | collective-permute-start | bytes 107528 | tf_op jit(solution)/shard_map/ppermute | solution.py:20
  443.4 37.0 %collective-permute-start.10 = (f32[4,35,64]{2,1,0:T(8,128)}, f32[4,35,64]{2,1,0:T(8,128)}, u32[]{:S(2)}, u32[]{:S(2)}) collective-permute-start(f32[4,35,64]{2,1,0:T(8,128)} %get-tuple-element.3084), channel_id=1, source_target_pairs={{0,2},{1,3},{2,4},{3,5},{4,6},{5,7},{6,8},{7,9},{8,10},{9,11},{10,... | collective-permute-start | bytes 107528 | tf_op jit(solution)/shard_map/ppermute | solution.py:20
  445.7 39.2 %collective-permute-start.11 = (f32[4,35,64]{2,1,0:T(8,128)}, f32[4,35,64]{2,1,0:T(8,128)}, u32[]{:S(2)}, u32[]{:S(2)}) collective-permute-start(f32[4,35,64]{2,1,0:T(8,128)} %get-tuple-element.3083), channel_id=1, source_target_pairs={{0,1},{1,2},{2,3},{3,4},{4,5},{5,6},{6,7},{7,8},{8,9},{9,10},{10,1... | collective-permute-start | bytes 107528 | tf_op jit(solution)/shard_map/ppermute | solution.py:20
  447.6 38.1 %collective-permute-start.12 = (f32[4,35,64]{2,1,0:T(8,128)}, f32[4,35,64]{2,1,0:T(8,128)}, u32[]{:S(2)}, u32[]{:S(2)}) collective-permute-start(f32[4,35,64]{2,1,0:T(8,128)} %get-tuple-element.3082), channel_id=1, source_target_pairs={{1,0},{2,1},{3,2},{4,3},{5,4},{6,5},{7,6},{8,7},{9,8},{10,9},{11,1... | collective-permute-start | bytes 107528 | tf_op jit(solution)/shard_map/ppermute | solution.py:20
  465.9 20.7 %collective-permute-start.13 = (f32[4,35,64]{2,1,0:T(8,128)}, f32[4,35,64]{2,1,0:T(8,128)S(1)}, u32[]{:S(2)}, u32[]{:S(2)}) collective-permute-start(f32[4,35,64]{2,1,0:T(8,128)} %get-tuple-element.3081), channel_id=1, source_target_pairs={{2,0},{3,1},{4,2},{5,3},{6,4},{7,5},{8,6},{9,7},{10,8},{11,9},{12,... | collective-permute-start | bytes 107528 | tf_op jit(solution)/shard_map/ppermute | solution.py:20
  474.0 12.7 %collective-permute-start.14 = (f32[4,35,64]{2,1,0:T(8,128)}, f32[4,35,64]{2,1,0:T(8,128)S(1)}, u32[]{:S(2)}, u32[]{:S(2)}) collective-permute-start(f32[4,35,64]{2,1,0:T(8,128)} %get-tuple-element.3080), channel_id=1, source_target_pairs={{3,0},{4,1},{5,2},{6,3},{7,4},{8,5},{9,6},{10,7},{11,8},{12,9},{13... | collective-permute-start | bytes 107528 | tf_op jit(solution)/shard_map/ppermute | solution.py:20
  480.3 8.0 collective-permute-start.15
  762.7 26.9 %collective-permute-start.16 = (f32[4,35,64]{2,1,0:T(8,128)}, f32[4,35,64]{2,1,0:T(8,128)}, u32[]{:S(2)}, u32[]{:S(2)}) collective-permute-start(f32[4,35,64]{2,1,0:T(8,128)} %get-tuple-element.3078), channel_id=1, source_target_pairs={{0,4},{1,5},{2,6},{3,7},{4,8},{5,9},{6,10},{7,11},{8,12},{9,13},{1... | collective-permute-start | bytes 107528 | tf_op jit(solution)/shard_map/ppermute | solution.py:20
  765.2 33.1 %collective-permute-start.17 = (f32[4,35,64]{2,1,0:T(8,128)}, f32[4,35,64]{2,1,0:T(8,128)}, u32[]{:S(2)}, u32[]{:S(2)}) collective-permute-start(f32[4,35,64]{2,1,0:T(8,128)} %get-tuple-element.3077), channel_id=1, source_target_pairs={{0,3},{1,4},{2,5},{3,6},{4,7},{5,8},{6,9},{7,10},{8,11},{9,12},{10... | collective-permute-start | bytes 107528 | tf_op jit(solution)/shard_map/ppermute | solution.py:20
  767.5 36.6 %collective-permute-start.18 = (f32[4,35,64]{2,1,0:T(8,128)}, f32[4,35,64]{2,1,0:T(8,128)}, u32[]{:S(2)}, u32[]{:S(2)}) collective-permute-start(f32[4,35,64]{2,1,0:T(8,128)} %get-tuple-element.3076), channel_id=1, source_target_pairs={{0,2},{1,3},{2,4},{3,5},{4,6},{5,7},{6,8},{7,9},{8,10},{9,11},{10,... | collective-permute-start | bytes 107528 | tf_op jit(solution)/shard_map/ppermute | solution.py:20
  769.4 41.1 %collective-permute-start.19 = (f32[4,35,64]{2,1,0:T(8,128)}, f32[4,35,64]{2,1,0:T(8,128)}, u32[]{:S(2)}, u32[]{:S(2)}) collective-permute-start(f32[4,35,64]{2,1,0:T(8,128)} %get-tuple-element.3075), channel_id=1, source_target_pairs={{0,1},{1,2},{2,3},{3,4},{4,5},{5,6},{6,7},{7,8},{8,9},{9,10},{10,1... | collective-permute-start | bytes 107528 | tf_op jit(solution)/shard_map/ppermute | solution.py:20
  771.3 40.1 %collective-permute-start.20 = (f32[4,35,64]{2,1,0:T(8,128)}, f32[4,35,64]{2,1,0:T(8,128)}, u32[]{:S(2)}, u32[]{:S(2)}) collective-permute-start(f32[4,35,64]{2,1,0:T(8,128)} %get-tuple-element.3074), channel_id=1, source_target_pairs={{1,0},{2,1},{3,2},{4,3},{5,4},{6,5},{7,6},{8,7},{9,8},{10,9},{11,1... | collective-permute-start | bytes 107528 | tf_op jit(solution)/shard_map/ppermute | solution.py:20
  789.6 22.7 %collective-permute-start.21 = (f32[4,35,64]{2,1,0:T(8,128)}, f32[4,35,64]{2,1,0:T(8,128)S(1)}, u32[]{:S(2)}, u32[]{:S(2)}) collective-permute-start(f32[4,35,64]{2,1,0:T(8,128)} %get-tuple-element.3073), channel_id=1, source_target_pairs={{2,0},{3,1},{4,2},{5,3},{6,4},{7,5},{8,6},{9,7},{10,8},{11,9},{12,... | collective-permute-start | bytes 107528 | tf_op jit(solution)/shard_map/ppermute | solution.py:20
  798.3 14.1 %collective-permute-start.22 = (f32[4,35,64]{2,1,0:T(8,128)}, f32[4,35,64]{2,1,0:T(8,128)S(1)}, u32[]{:S(2)}, u32[]{:S(2)}) collective-permute-start(f32[4,35,64]{2,1,0:T(8,128)} %get-tuple-element.3072), channel_id=1, source_target_pairs={{3,0},{4,1},{5,2},{6,3},{7,4},{8,5},{9,6},{10,7},{11,8},{12,9},{13... | collective-permute-start | bytes 107528 | tf_op jit(solution)/shard_map/ppermute | solution.py:20
  804.1 8.3 collective-permute-start.23
  1005.5 24.3 %collective-permute-start.24 = (f32[4,35,64]{2,1,0:T(8,128)}, f32[4,35,64]{2,1,0:T(8,128)}, u32[]{:S(2)}, u32[]{:S(2)}) collective-permute-start(f32[4,35,64]{2,1,0:T(8,128)} %get-tuple-element.3070), channel_id=1, source_target_pairs={{0,4},{1,5},{2,6},{3,7},{4,8},{5,9},{6,10},{7,11},{8,12},{9,13},{1... | collective-permute-start | bytes 107528 | tf_op jit(solution)/shard_map/ppermute | solution.py:20
  1008.1 30.1 %collective-permute-start.25 = (f32[4,35,64]{2,1,0:T(8,128)}, f32[4,35,64]{2,1,0:T(8,128)}, u32[]{:S(2)}, u32[]{:S(2)}) collective-permute-start(f32[4,35,64]{2,1,0:T(8,128)} %get-tuple-element.3069), channel_id=1, source_target_pairs={{0,3},{1,4},{2,5},{3,6},{4,7},{5,8},{6,9},{7,10},{8,11},{9,12},{10... | collective-permute-start | bytes 107528 | tf_op jit(solution)/shard_map/ppermute | solution.py:20
  1010.0 34.5 %collective-permute-start.26 = (f32[4,35,64]{2,1,0:T(8,128)}, f32[4,35,64]{2,1,0:T(8,128)}, u32[]{:S(2)}, u32[]{:S(2)}) collective-permute-start(f32[4,35,64]{2,1,0:T(8,128)} %get-tuple-element.3068), channel_id=1, source_target_pairs={{0,2},{1,3},{2,4},{3,5},{4,6},{5,7},{6,8},{7,9},{8,10},{9,11},{10,... | collective-permute-start | bytes 107528 | tf_op jit(solution)/shard_map/ppermute | solution.py:20
  1012.0 38.8 %collective-permute-start.27 = (f32[4,35,64]{2,1,0:T(8,128)}, f32[4,35,64]{2,1,0:T(8,128)}, u32[]{:S(2)}, u32[]{:S(2)}) collective-permute-start(f32[4,35,64]{2,1,0:T(8,128)} %get-tuple-element.3067), channel_id=1, source_target_pairs={{0,1},{1,2},{2,3},{3,4},{4,5},{5,6},{6,7},{7,8},{8,9},{9,10},{10,1... | collective-permute-start | bytes 107528 | tf_op jit(solution)/shard_map/ppermute | solution.py:20
  1013.9 37.8 %collective-permute-start.28 = (f32[4,35,64]{2,1,0:T(8,128)}, f32[4,35,64]{2,1,0:T(8,128)}, u32[]{:S(2)}, u32[]{:S(2)}) collective-permute-start(f32[4,35,64]{2,1,0:T(8,128)} %get-tuple-element.3066), channel_id=1, source_target_pairs={{1,0},{2,1},{3,2},{4,3},{5,4},{6,5},{7,6},{8,7},{9,8},{10,9},{11,1... | collective-permute-start | bytes 107528 | tf_op jit(solution)/shard_map/ppermute | solution.py:20
  1029.7 22.8 %collective-permute-start.29 = (f32[4,35,64]{2,1,0:T(8,128)}, f32[4,35,64]{2,1,0:T(8,128)S(1)}, u32[]{:S(2)}, u32[]{:S(2)}) collective-permute-start(f32[4,35,64]{2,1,0:T(8,128)} %get-tuple-element.3065), channel_id=1, source_target_pairs={{2,0},{3,1},{4,2},{5,3},{6,4},{7,5},{8,6},{9,7},{10,8},{11,9},{12,... | collective-permute-start | bytes 107528 | tf_op jit(solution)/shard_map/ppermute | solution.py:20
  1038.2 14.4 %collective-permute-start.30 = (f32[4,35,64]{2,1,0:T(8,128)S(1)}, f32[4,35,64]{2,1,0:T(8,128)S(1)}, u32[]{:S(2)}, u32[]{:S(2)}) collective-permute-start(f32[4,35,64]{2,1,0:T(8,128)S(1)} %copy-done.73), channel_id=1, source_target_pairs={{3,0},{4,1},{5,2},{6,3},{7,4},{8,5},{9,6},{10,7},{11,8},{12,9},{13... | collective-permute-start | bytes 107528 | tf_op jit(solution)/shard_map/ppermute | solution.py:20
  1044.5 8.1 collective-permute-start.31
  (186 other events, 2642.9 us)
where the time goes:
time: 1120 us; the launch traced here: 1100 us
  local copies, waits for them, and re-layouts  556 us (50%)
  matrix products  242 us (22%)
  other arithmetic  160 us (14%)
  starting transfers between devices  118 us (11%)
  loops' own time  12.6 us (1%)
    ppermute x32, starting transfers between devices, passed_along(): lax.ppermute(value, axis, [(source, source + steps) for source in range(l...  118 us
    dot_general x40, matrix products, derivative_rows(): jnp.einsum('jie,jiae->ae', inv_jacobian, mixed[:, 1:], precision=HIGH)  114 us
    slice x80, local copies, waits for them, and re-layouts, derivative_rows(): mixed[:, 1:]  100 us
    dot_general x40, matrix products, derivative_rows(): jnp.einsum('jie,jae->iae', inv_jacobian, mixed[:, 0], precision=HIGH)  82.5 us
    gather x48, local copies, waits for them, and re-layouts, rotate_faces(): raw_traces[:, order_table[turn_index], :]  81.3 us
    squeeze x80, local copies, waits for them, and re-layouts, derivative_rows(): mixed[:, 0]  57.7 us
    gather x8, local copies, waits for them, and re-layouts, body(): local_part = jnp.where(local_live, traced[:, :, local_source], 0.0)  46.9 us
    gather x8, local copies, waits for them, and re-layouts, body(): received_flat[:, :, remote_source]  41.6 us
  transfers between devices with their start and end apart: 32, of which 2 were waited for; matrix products, arithmetic and copies ran while one was open for 8% of the time, Pallas kernels for 0%

commit v1 on v0

v1 whole, which is shorter than its diff:
```python
import math

import jax
import jax.numpy as jnp
import numpy as np
from jax import lax
from jax.experimental import pallas as pl
from jax.experimental.pallas import tpu as pltpu
from jax.sharding import PartitionSpec as P

SUBSTEPS = 4
STEP_LENGTH = 0.3
QUANT = 4
BASIS = 35
ROWS = 40
NODES = 15
NROWS = 16
ELEMS = 256
FACES = 4 * ELEMS
OFFSETS = 8
CAP = 64
SLOTS = OFFSETS * CAP
F32, BF16 = jnp.float32, jnp.bfloat16
PAIRS = ((0, 0), (1, 1), (2, 2), (0, 1), (0, 2), (1, 2))


def node_orders():
    nodes = [(i, j) for i in range(5) for j in range(5 - i)]
    place = {node: position for position, node in enumerate(nodes)}
    turns = [(0, 1, 2), (1, 2, 0), (2, 0, 1), (0, 2, 1), (2, 1, 0), (1, 0, 2)]
    table = []
    for turn in turns:
        row = []
        for node in nodes:
            corner = (node[0], node[1], 4 - node[0] - node[1])
            row.append(place[corner[turn[0]], corner[turn[1]]])
        table.append(row)
    return table


def turn_matrix():
    out = np.zeros((6 * NROWS, 128), np.float32)
    for t, row in enumerate(node_orders()):
        for n, source in enumerate(row):
            out[t * NROWS + n, source] = 1.0
    return out


def dot(a, b):
    return lax.dot_general(a, b, (((1,), (0,)), ((), ())), preferred_element_type=F32)


def exact_dot(a, b):
    return lax.dot_general(
        a, b, (((1,), (0,)), ((), ())), precision=lax.Precision.HIGHEST, preferred_element_type=F32
    )


def halves(x):
    hi = x.astype(BF16).astype(F32)
    return hi, x - hi


def stack3(x):
    hi, lo = halves(x)
    return jnp.concatenate([hi, lo, hi, jnp.zeros((8, x.shape[1]), F32)], axis=0).astype(BF16)


def left3(a):
    hi, lo = halves(a)
    return (hi + pltpu.roll(hi, 40, 1) + pltpu.roll(lo, 80, 1)).astype(BF16)


def kernel(
    n_dev,
    dofs, cluster, neighbours, orientation, send_slots, recv_slots, jac, normals, area, bulk, invd,
    deriv, proj, turns, out,
    u_s, a_s, own_s, near_s, pad_s, fpad_s, grad_s, gradt_s, div_s, divt_s, second_s,
    trace_s, lift_s, choose_s, pick_send, pick_local, place_recv, slot_s, zn_s, zline_s,
    zslot_s, code_send, code_local, face_recv, coef_s, tell_out, tell_in, send_buf, recv_buf,
    tell_send, tell_recv, send_sem, recv_sem,
):
    me = lax.axis_index("dom")
    steps = [k - 4 if k < 4 else k - 3 for k in range(OFFSETS)]
    partner = [lax.rem(me + (step + n_dev), n_dev) for step in steps]
    barrier = pltpu.get_barrier_semaphore()
    for k in range(OFFSETS):
        pl.semaphore_signal(
            barrier, inc=1, device_id=(partner[k],), device_id_type=pl.DeviceIdType.MESH
        )

    low = lax.broadcasted_iota(jnp.int32, (8, 128), 1) < CAP
    low1 = lax.broadcasted_iota(jnp.int32, (1, 128), 1) < CAP

    slot_s[...] = jnp.zeros((16, 128), jnp.int32)
    slot_s[0:8, 0:CAP] = send_slots[...]
    slot_s[8:16, 0:CAP] = recv_slots[...]
    both = slot_s[...]
    both = both + pltpu.roll(both, CAP, 1)

    def slot_row(first):
        tiles = [
            jnp.where(
                low1,
                both[first + 2 * p : first + 2 * p + 1],
                both[first + 2 * p + 1 : first + 2 * p + 2],
            )
            for p in range(4)
        ]
        row = jnp.concatenate(tiles, axis=1)
        one, zero = jnp.ones_like(row), jnp.zeros_like(row)
        face = (
            jnp.where(row >= ELEMS, one, zero)
            + jnp.where(row >= 2 * ELEMS, one, zero)
            + jnp.where(row >= 3 * ELEMS, one, zero)
        )
        elem = jnp.where(row >= 0, row - face * ELEMS, -one)
        face = jnp.where(row >= 0, face, -one)
        return face, elem

    send_face, send_elem = slot_row(0)
    recv_face, recv_elem = slot_row(8)

    bulk_r, invd_r = bulk[...], invd[...]
    imp = jnp.sqrt(bulk_r / invd_r)
    code = orientation[...]
    one4, zero4 = jnp.ones_like(code), jnp.zeros_like(code)
    turn_f = (
        code
        - 6 * jnp.where(code >= 6, one4, zero4)
        - 6 * jnp.where(code >= 12, one4, zero4)
        - 6 * jnp.where(code >= 18, one4, zero4)
    ).astype(F32)
    table = []
    for f in range(4):
        zn = normals[f] * imp
        for i in range(3):
            zline_s[i : i + 1, f * ELEMS : (f + 1) * ELEMS] = zn[i : i + 1]
        zn_s[f] = jnp.zeros((8, ELEMS), F32)
        zn_s[f, 0:3] = zn
        zn_s[f, 3:4] = turn_f[f : f + 1]
        code_local[:, f * ELEMS : (f + 1) * ELEMS] = jnp.broadcast_to(code[f : f + 1], (8, ELEMS))
        table.append(zn_s[f])
    table = jnp.concatenate(table, axis=0)
    t_hi, t_rest = halves(table)
    t_mid, t_lo = halves(t_rest)
    table = jnp.concatenate([t_hi, t_mid, t_lo], axis=0).astype(BF16)
    elem_rows = lax.broadcasted_iota(jnp.int32, (ELEMS, SLOTS), 0)
    seen = dot(table, jnp.where(elem_rows == recv_elem, 1.0, 0.0).astype(BF16))
    seen = seen[0:32] + seen[32:64] + seen[64:96]
    tell = jnp.zeros((8, SLOTS), F32)
    for f in range(4):
        tell = jnp.where(recv_face == f, seen[8 * f : 8 * f + 8], tell)
    for k in range(OFFSETS):
        tell_out[k] = tell[:, (k // 2) * 128 : (k // 2 + 1) * 128]

    pl.semaphore_wait(barrier, OFFSETS)

    def tell_copy(k):
        return pltpu.make_async_remote_copy(
            src_ref=tell_out.at[k],
            dst_ref=tell_in.at[OFFSETS - 1 - k],
            send_sem=tell_send.at[k],
            recv_sem=tell_recv.at[OFFSETS - 1 - k],
            device_id=(partner[k],),
            device_id_type=pl.DeviceIdType.MESH,
        )

    for k in range(OFFSETS):
        tell_copy(k).start()

    pick = jnp.where(elem_rows == send_elem, 1.0, 0.0).astype(BF16)
    pick_send[0:ELEMS] = pick
    pick_send[ELEMS:] = pick
    elem_rows1 = lax.broadcasted_iota(jnp.int32, (ELEMS, ELEMS), 0)
    for f in range(4):
        pick = jnp.where(elem_rows1 == neighbours[f : f + 1], 1.0, 0.0).astype(BF16)
        pick_local[0:ELEMS, f * ELEMS : (f + 1) * ELEMS] = pick
        pick_local[ELEMS:, f * ELEMS : (f + 1) * ELEMS] = pick
    elem_lanes = lax.broadcasted_iota(jnp.int32, (128, ELEMS), 1).astype(F32)
    recv_float = recv_elem.astype(F32)
    for p in range(4):
        column = jnp.broadcast_to(recv_float[:, p * 128 : (p + 1) * 128], (128, 128)).T
        column = jnp.concatenate([column, column], axis=1)
        place_recv[p * 128 : (p + 1) * 128] = jnp.where(column == elem_lanes, 1.0, 0.0).astype(BF16)
    face_recv[...] = jnp.broadcast_to(recv_face, (8, SLOTS))

    pad_s[...] = jnp.zeros_like(pad_s)
    fpad_s[...] = jnp.zeros_like(fpad_s)
    for j in range(3):
        pad_s[j, 0:BASIS, 0:BASIS] = deriv[j]
    for f in range(4):
        fpad_s[f, 0:NODES, 0:BASIS] = proj[f]
    d = [pad_s[j] for j in range(3)]
    grad = jnp.concatenate([m[0:ROWS] for m in d], axis=0)
    dt = [m.T for m in d]
    gradt = jnp.concatenate([m[0:ROWS] for m in dt], axis=0)
    grad_s[...] = left3(grad)
    gradt_s[...] = left3(gradt)
    for ref, mats in ((div_s, d), (divt_s, dt)):
        wide = (
            mats[0][0:ROWS]
            + pltpu.roll(mats[1][0:ROWS], 40, 1)
            + pltpu.roll(mats[2][0:ROWS], 80, 1)
        )
        hi, lo = halves(wide)
        ref[...] = jnp.concatenate([hi, hi, lo], axis=1).astype(BF16)
    products = [exact_dot(grad, d[k]) for k in range(3)]
    second = []
    for j, k in PAIRS:
        term = products[k][j * ROWS : (j + 1) * ROWS]
        if j != k:
            term = term + products[j][k * ROWS : (k + 1) * ROWS]
        second.append(term)
    second_s[...] = left3(jnp.concatenate(second, axis=0))
    faces = jnp.concatenate([fpad_s[f, 0:NROWS] for f in range(4)], axis=0)
    trace_s[...] = left3(faces)
    lifts = jnp.concatenate([faces, jnp.zeros((64, 128), F32)], axis=0).T[0:ROWS]
    hi, lo = halves(lifts)
    lift_s[...] = jnp.concatenate(
        [hi + pltpu.roll(hi, 64, 1), lo + pltpu.roll(lo, 64, 1)], axis=1
    ).astype(BF16)
    turn_rows = turns[...]
    for f in range(4):
        choose_s[f * 96 : (f + 1) * 96] = left3(exact_dot(turn_rows, fpad_s[f]))

    kappa = bulk_r * invd_r
    g = [[jac[j, i : i + 1, :] for i in range(3)] for j in range(3)]
    for j in range(3):
        for i in range(3):
            coef_s[3 * j + i : 3 * j + i + 1] = g[j][i]
            coef_s[9 + 3 * j + i : 10 + 3 * j + i] = -invd_r * g[j][i]
    for c, (j, k) in enumerate(PAIRS):
        coef_s[18 + c : 19 + c] = kappa * (
            g[j][0] * g[k][0] + g[j][1] * g[k][1] + g[j][2] * g[k][2]
        )
    for f in range(4):
        size = area[f : f + 1]
        coef_s[24 + f : 25 + f] = 0.5 * size * bulk_r / imp
        for i in range(3):
            row = 28 + 3 * f + i
            coef_s[row : row + 1] = 0.5 * size * invd_r * normals[f, i : i + 1]

    u_s[...] = jnp.zeros_like(u_s)
    for q in range(QUANT):
        u_s[q, 0:BASIS] = dofs[q]
    a_s[...] = jnp.zeros_like(a_s)
    near_s[...] = jnp.zeros_like(near_s)
    own_s[...] = jnp.zeros_like(own_s)

    def coef(row):
        return coef_s[row : row + 1]

    for k in range(OFFSETS):
        tell_copy(k).wait()
    for p in range(4):
        tile = pltpu.roll(jnp.where(low, tell_in[2 * p + 1], tell_in[2 * p]), CAP, 1)
        zslot_s[:, p * 128 : (p + 1) * 128] = tile
    code_send[...] = jnp.broadcast_to(
        send_face * 6 + zslot_s[3:4].astype(jnp.int32), (8, SLOTS)
    )

    def chosen(parts, codes):
        first = jnp.zeros((8, codes.shape[1]), F32)
        second = first
        for c in range(24):
            mask = codes == c
            first = jnp.where(mask, parts[c * 16 : c * 16 + 8], first)
            second = jnp.where(mask, parts[c * 16 + 8 : c * 16 + 16], second)
        return first, second

    def step(s, carry):
        kind = cluster[...]
        s_vec = jnp.full(kind.shape, 0, jnp.int32) + s
        odd = jnp.bitwise_and(s_vec, 1)
        zero = jnp.zeros_like(kind)
        phase = jnp.where(kind == 0, zero, jnp.where(kind == 1, odd, s_vec))
        begin = phase.astype(F32) * STEP_LENGTH
        finish = begin + STEP_LENGTH
        b_pow, f_pow, c = begin, finish, []
        for k in range(5):
            c.append((f_pow - b_pow) * (1.0 / math.factorial(k + 1)))
            b_pow, f_pow = b_pow * begin, f_pow * finish
        left = jnp.where(
            kind == 0, zero, jnp.where(kind == 1, 1 - odd, jnp.bitwise_and(s_vec + 1, 3))
        )
        done = left == 0

        p0 = u_s[0]
        u = [u_s[i + 1] for i in range(3)]

        def contra(v):
            return [
                coef(3 * j) * v[0] + coef(3 * j + 1) * v[1] + coef(3 * j + 2) * v[2]
                for j in range(3)
            ]

        def stack_div(w):
            parts = [halves(x) for x in w]
            pad = jnp.zeros((8, ELEMS), F32)
            his = [p[0] for p in parts] + [pad]
            los = [p[1] for p in parts] + [pad]
            return jnp.concatenate(his + los + his, axis=0).astype(BF16)

        def twice(e):
            total = coef(18) * e[0:ROWS]
            for c_at in range(1, 6):
                total = total + coef(18 + c_at) * e[c_at * ROWS : (c_at + 1) * ROWS]
            return total

        bulk_now, invd_now = bulk[...], invd[...]
        p1 = -bulk_now * dot(div_s[...], stack_div(contra(u)))
        p2 = twice(dot(second_s[...], stack3(p0)))
        e12 = dot(second_s[...], jnp.concatenate([stack3(p1), stack3(p2)], axis=1))
        p3, p4 = twice(e12[:, 0:ELEMS]), twice(e12[:, ELEMS:])
        slope = dot(grad_s[...], stack3(c[1] * p0 + c[2] * p1 + c[3] * p2 + c[4] * p3))
        j_all = [c[0] * p0 + c[1] * p1 + c[2] * p2 + c[3] * p3 + c[4] * p4]
        for i in range(3):
            total = c[0] * u[i]
            for j in range(3):
                total = total + coef(9 + 3 * j + i) * slope[j * ROWS : (j + 1) * ROWS]
            j_all.append(total)
        parts = [halves(x) for x in j_all]
        j_two = jnp.concatenate(
            [
                jnp.concatenate([p[0] for p in parts], axis=0),
                jnp.concatenate([p[1] for p in parts], axis=0),
            ],
            axis=1,
        ).astype(BF16)

        at_slot = dot(j_two, pick_send[...])
        mix = at_slot[0:ROWS]
        for i in range(3):
            mix = mix - zslot_s[i : i + 1] * at_slot[(i + 1) * ROWS : (i + 2) * ROWS]
        first, second = chosen(dot(choose_s[...], stack3(mix)), code_send[...])
        for p in range(4):
            x0 = first[:, p * 128 : (p + 1) * 128]
            x1 = pltpu.roll(second[:, p * 128 : (p + 1) * 128], CAP, 1)
            send_buf[s, 2 * p] = jnp.where(low, x0, x1)
            send_buf[s, 2 * p + 1] = jnp.where(low, x1, x0)

        def trace_copy(k):
            return pltpu.make_async_remote_copy(
                src_ref=send_buf.at[s, k],
                dst_ref=recv_buf.at[s, OFFSETS - 1 - k],
                send_sem=send_sem.at[s, k],
                recv_sem=recv_sem.at[s, OFFSETS - 1 - k],
                device_id=(partner[k],),
                device_id_type=pl.DeviceIdType.MESH,
            )

        for k in range(OFFSETS):
            trace_copy(k).start()

        at_face = dot(j_two, pick_local[...])
        mix = at_face[0:ROWS]
        for i in range(3):
            mix = mix - zline_s[i : i + 1] * at_face[(i + 1) * ROWS : (i + 2) * ROWS]
        first, second = chosen(dot(choose_s[...], stack3(mix)), code_local[...])
        traced = dot(trace_s[...], jnp.concatenate([stack3(x) for x in j_all], axis=1))
        for f in range(4):
            rows = slice(f * NROWS, (f + 1) * NROWS)
            near_s[f * NROWS : f * NROWS + 8] += first[:, f * ELEMS : (f + 1) * ELEMS]
            near_s[f * NROWS + 8 : f * NROWS + 16] += second[:, f * ELEMS : (f + 1) * ELEMS]
            mine = traced[rows, 0:ELEMS]
            for i in range(3):
                mine = mine + zn_s[f, i : i + 1] * traced[rows, (i + 1) * ELEMS : (i + 2) * ELEMS]
            a_s[rows] += mine
        own = [own_s[q] + j_all[q] for q in range(QUANT)]
        change_p = bulk_now * dot(divt_s[...], stack_div(contra(own[1:])))
        slope = dot(gradt_s[...], stack3(own[0]))
        change = [change_p]
        for i in range(3):
            total = coef(9 + i) * slope[0:ROWS]
            for j in range(1, 3):
                total = total + coef(9 + 3 * j + i) * slope[j * ROWS : (j + 1) * ROWS]
            change.append(-total)
        for q in range(QUANT):
            own_s[q] = jnp.where(done, 0.0, own[q])
            u_s[q] = jnp.where(done, u_s[q] + change[q], u_s[q])

        for k in range(OFFSETS):
            trace_copy(k).wait()
        r0, r1 = [], []
        for p in range(4):
            even, odd_block = recv_buf[s, 2 * p], recv_buf[s, 2 * p + 1]
            r0.append(pltpu.roll(jnp.where(low, odd_block, even), CAP, 1))
            r1.append(jnp.where(low, even, odd_block))
        r0, r1 = jnp.concatenate(r0, axis=1), jnp.concatenate(r1, axis=1)
        r0h, r0l = halves(r0)
        r1h, r1l = halves(r1)
        slot_face = face_recv[...]
        his, los = [], []
        for f in range(4):
            mask = slot_face == f
            his += [jnp.where(mask, r0h, 0.0), jnp.where(mask, r1h, 0.0)]
            los += [jnp.where(mask, r0l, 0.0), jnp.where(mask, r1l, 0.0)]
        placed = dot(jnp.concatenate(his + los, axis=0).astype(BF16), place_recv[...])
        near_all = near_s[...] + placed[0:64] + placed[64:128]
        a_all = a_s[...]
        near_s[...] = jnp.where(done, 0.0, near_all)
        a_s[...] = jnp.where(done, 0.0, a_all)

        flux = [[], [], [], []]
        for f in range(4):
            rows = slice(f * NROWS, (f + 1) * NROWS)
            own_f = a_all[rows]
            far_f = jnp.where(neighbours[f : f + 1] == -1, own_f, near_all[rows])
            flux[0].append(coef(24 + f) * (own_f - far_f))
            plus = own_f + far_f
            for i in range(3):
                flux[i + 1].append(coef(28 + 3 * f + i) * plus)
        flux = jnp.concatenate([jnp.concatenate(rows, axis=0) for rows in flux], axis=1)
        hi, lo = halves(flux)
        lifted = dot(lift_s[...], jnp.concatenate([hi, lo, hi, lo], axis=0).astype(BF16))
        for q in range(QUANT):
            part = lifted[:, q * ELEMS : (q + 1) * ELEMS]
            u_s[q] = jnp.where(done, u_s[q] - part, u_s[q])
        return carry

    lax.fori_loop(0, SUBSTEPS, step, 0)
    for q in range(QUANT):
        out[q] = u_s[q, 0:BASIS]


def body(
    initial_dofs, cluster, neighbours, orientation, send_slots, recv_slots, inv_jacobian, normals,
    face_area, bulk_modulus, inv_density, deriv_mats, face_proj,
):
    n_dev = lax.axis_size("dom")
    vmem = pl.BlockSpec(memory_space=pltpu.VMEM)

    def call(*operands):
        return pl.pallas_call(
            lambda *refs: kernel(n_dev, *refs),
            out_shape=jax.ShapeDtypeStruct((QUANT, BASIS, ELEMS), F32),
            in_specs=[vmem] * len(operands),
            out_specs=vmem,
            scratch_shapes=[
                pltpu.VMEM((QUANT, ROWS, ELEMS), F32),
                pltpu.VMEM((4 * NROWS, ELEMS), F32),
                pltpu.VMEM((QUANT, ROWS, ELEMS), F32),
                pltpu.VMEM((4 * NROWS, ELEMS), F32),
                pltpu.VMEM((3, 128, 128), F32),
                pltpu.VMEM((4, 128, 128), F32),
                pltpu.VMEM((3 * ROWS, 128), BF16),
                pltpu.VMEM((3 * ROWS, 128), BF16),
                pltpu.VMEM((ROWS, 384), BF16),
                pltpu.VMEM((ROWS, 384), BF16),
                pltpu.VMEM((6 * ROWS, 128), BF16),
                pltpu.VMEM((4 * NROWS, 128), BF16),
                pltpu.VMEM((ROWS, 256), BF16),
                pltpu.VMEM((24 * NROWS, 128), BF16),
                pltpu.VMEM((2 * ELEMS, SLOTS), BF16),
                pltpu.VMEM((2 * ELEMS, FACES), BF16),
                pltpu.VMEM((SLOTS, ELEMS), BF16),
                pltpu.VMEM((16, 128), jnp.int32),
                pltpu.VMEM((4, 8, ELEMS), F32),
                pltpu.VMEM((8, FACES), F32),
                pltpu.VMEM((8, SLOTS), F32),
                pltpu.VMEM((8, SLOTS), jnp.int32),
                pltpu.VMEM((8, FACES), jnp.int32),
                pltpu.VMEM((8, SLOTS), jnp.int32),
                pltpu.VMEM((40, ELEMS), F32),
                pltpu.VMEM((OFFSETS, 8, 128), F32),
                pltpu.VMEM((OFFSETS, 8, 128), F32),
                pltpu.VMEM((SUBSTEPS, OFFSETS, 8, 128), F32),
                pltpu.VMEM((SUBSTEPS, OFFSETS, 8, 128), F32),
                pltpu.SemaphoreType.DMA((OFFSETS,)),
                pltpu.SemaphoreType.DMA((OFFSETS,)),
                pltpu.SemaphoreType.DMA((SUBSTEPS, OFFSETS)),
                pltpu.SemaphoreType.DMA((SUBSTEPS, OFFSETS)),
            ],
            compiler_params=pltpu.CompilerParams(
                collective_id=0, has_side_effects=True, vmem_limit_bytes=48 * 1024 * 1024
            ),
        )(*operands)

    return call(
        initial_dofs,
        cluster.reshape(1, ELEMS),
        neighbours,
        orientation,
        send_slots,
        recv_slots,
        inv_jacobian,
        normals,
        face_area,
        bulk_modulus.reshape(1, ELEMS),
        inv_density.reshape(1, ELEMS),
        deriv_mats,
        face_proj,
        jnp.asarray(turn_matrix()),
    )


def solution(mesh):
    return jax.shard_map(
        body,
        mesh=mesh,
        in_specs=(
            P(None, None, "dom"),
            P("dom"),
            P(None, "dom"),
            P(None, "dom"),
            P(None, "dom"),
            P(None, "dom"),
            P(None, None, "dom"),
            P(None, None, "dom"),
            P(None, "dom"),
            P("dom"),
            P("dom"),
            P(),
            P(),
        ),
        out_specs=P(None, None, "dom"),
        check_vma=False,
    )
```

time: 1120 us -> 44.8 us (0.04)
  the two profiles are of different devices: /device:TPU:25 before, /device:TPU:1 now
where the time goes in v1:
time: 44.8 us; the launch traced here: 44.6 us
  Pallas kernels  41.9 us (94%)
  local copies, waits for them, and re-layouts  2.57 us (6%)
    pallas_call x1, Pallas kernels, call(): pl.pallas_call(lambda *refs: kernel(n_dev, *refs), out_shape=jax.ShapeDty...  41.9 us
    unnamed x27, local copies, waits for them, and re-layouts  1.85 us

profile of v1, /device:TPU:1, one launch (start us, length us, event | category | flops | bytes accessed | tf_op | source)
XLA Modules:
  0.0 44.6 jit_solution(4765591788378440958)
XLA Ops:
  0.0 0.0 copy-start.11
  0.0 0.7 %copy.16.refs_7_ = f32[4,3,256]{2,1,0:T(4,128)S(1)} copy(f32[4,3,256]{2,0,1:T(4,128)} %param.21) | data formatting | bytes 24576 | tf_op args[7]
  0.7 0.0 copy-done.11
  0.8 0.0 copy-start
  0.8 0.0 copy-start.1
  0.8 0.0 copy-start.2
  0.8 0.0 copy-start.3
  0.8 0.0 copy-start.4
  0.8 0.0 copy-start.5
  0.8 0.0 copy-start.6
  0.8 0.0 copy-start.7
  0.9 0.0 copy-start.8
  0.9 0.0 copy-start.9
  0.9 0.0 copy-start.10
  0.9 1.0 %copy.15.refs_0_ = f32[4,35,256]{2,1,0:T(8,128)S(1)} copy(f32[4,35,256]{2,0,1:T(4,128)} %param.14) | data formatting | bytes 286720 | tf_op args[0]
  1.9 0.0 copy-done
  1.9 0.0 copy-done.1
  1.9 0.0 copy-done.2
  1.9 0.0 copy-done.3
  1.9 0.0 copy-done.4
  2.0 0.0 copy-done.5
  2.0 0.0 copy-done.6
  2.0 0.0 copy-done.7
  2.0 0.0 copy-done.8
  2.0 0.0 copy-done.9
  2.0 0.0 copy-done.10
  2.0 41.9 %shard_map.136 = f32[4,35,256]{2,1,0:T(8,128)S(1)} custom-call(f32[4,35,256]{2,1,0:T(8,128)S(1)} %copy.15.refs_0_, s32[1,256]{1,0:T(1,128)S(1)} %bitcast.3, s32[4,256]{1,0:T(4,128)S(1)} %copy-done.3, s32[4,256]{1,0:T(4,128)S(1)} %copy-done.4, s32[8,64]{1,0:T(8,128)S(1)} %copy-done.5, s32[8,64]{1,0:T(8,128)S(1)} %copy-done.6, f32[3,3,256]{2,1,0:T(4,128)S(1)} %copy-done.2, ...), custom_call_target="tpu_custom_call" | custom-call | tf_op jit(solution)/shard_map/pallas_call | solution.py:435
  43.9 0.7 %copy.18 = f32[4,35,256]{2,0,1:T(4,128)} copy(f32[4,35,256]{2,1,0:T(8,128)S(1)} %shard_map.136) | data formatting | bytes 286720 | tf_op jit(solution)/shard_map/pallas_call | solution.py:435
  (1 shorter events, 0.0 us)
Async XLA Ops:
  0.0 0.8 %copy-start.11 = (f32[4,15,35]{2,0,1:T(4,128)S(1)}, f32[4,15,35]{2,0,1:T(4,128)}, u32[]{:S(2)}) copy-start(f32[4,15,35]{2,0,1:T(4,128)} %param.26) | copy-start | bytes 25204
  0.8 1.1 %copy-start = (f32[3,35,35]{2,1,0:T(8,128)S(1)}, f32[3,35,35]{2,1,0:T(8,128)}, u32[]{:S(2)}) copy-start(f32[3,35,35]{2,1,0:T(8,128)} %refs_11_.1) | copy-start | bytes 44104
  0.8 1.1 %copy-start.1 = (f32[96,128]{1,0:T(8,128)S(1)}, f32[96,128]{1,0:T(8,128)}, u32[]{:S(2)}) copy-start(f32[96,128]{1,0:T(8,128)} %constant.2.clone.refs_13_) | copy-start | bytes 147460
  0.8 1.1 %copy-start.2 = (f32[3,3,256]{2,1,0:T(4,128)S(1)}, f32[3,3,256]{2,1,0:T(4,128)}, u32[]{:S(2)}) copy-start(f32[3,3,256]{2,1,0:T(4,128)} %refs_6_.1) | copy-start | bytes 27652
  0.8 1.1 %copy-start.3 = (s32[4,256]{1,0:T(4,128)S(1)}, s32[4,256]{1,0:T(4,128)}, u32[]{:S(2)}) copy-start(s32[4,256]{1,0:T(4,128)} %refs_2_.1) | copy-start | bytes 12292
  0.8 1.1 %copy-start.4 = (s32[4,256]{1,0:T(4,128)S(1)}, s32[4,256]{1,0:T(4,128)}, u32[]{:S(2)}) copy-start(s32[4,256]{1,0:T(4,128)} %refs_3_.1) | copy-start | bytes 12292
  0.8 1.1 %copy-start.5 = (s32[8,64]{1,0:T(8,128)S(1)}, s32[8,64]{1,0:T(8,128)}, u32[]{:S(2)}) copy-start(s32[8,64]{1,0:T(8,128)} %refs_4_.1) | copy-start | bytes 6148
  0.8 1.1 %copy-start.6 = (s32[8,64]{1,0:T(8,128)S(1)}, s32[8,64]{1,0:T(8,128)}, u32[]{:S(2)}) copy-start(s32[8,64]{1,0:T(8,128)} %refs_5_.1) | copy-start | bytes 6148
  0.8 1.1 %copy-start.7 = (f32[4,256]{1,0:T(4,128)S(1)}, f32[4,256]{1,0:T(4,128)}, u32[]{:S(2)}) copy-start(f32[4,256]{1,0:T(4,128)} %refs_8_.1) | copy-start | bytes 12292
  0.9 1.1 %copy-start.8 = (s32[256]{0:T(256)S(1)}, s32[256]{0:T(256)}, u32[]{:S(2)}) copy-start(s32[256]{0:T(256)} %param.15) | copy-start | bytes 3076
  0.9 1.1 %copy-start.9 = (f32[256]{0:T(256)S(1)}, f32[256]{0:T(256)}, u32[]{:S(2)}) copy-start(f32[256]{0:T(256)} %param.23) | copy-start | bytes 3076
  0.9 1.1 %copy-start.10 = (f32[256]{0:T(256)S(1)}, f32[256]{0:T(256)}, u32[]{:S(2)}) copy-start(f32[256]{0:T(256)} %param.24) | copy-start | bytes 3076

commit v2 on v1

v2 whole, which is shorter than its diff:
```python
import math

import jax
import jax.numpy as jnp
import numpy as np
from jax import lax
from jax.experimental import pallas as pl
from jax.experimental.pallas import tpu as pltpu
from jax.sharding import PartitionSpec as P

SUBSTEPS = 4
STEP_LENGTH = 0.3
QUANT = 4
BASIS = 35
ROWS = 40
NODES = 15
NROWS = 16
ELEMS = 256
FACES = 4 * ELEMS
OFFSETS = 8
CAP = 64
SLOTS = OFFSETS * CAP
F32, BF16 = jnp.float32, jnp.bfloat16
TILES = (0, 3, 1, 2)
FAR_FIRST = (0, 7, 1, 6, 2, 5, 3, 4)
PAIRS = ((0, 0), (1, 1), (2, 2), (0, 1), (0, 2), (1, 2))


def node_orders():
    nodes = [(i, j) for i in range(5) for j in range(5 - i)]
    place = {node: position for position, node in enumerate(nodes)}
    turns = [(0, 1, 2), (1, 2, 0), (2, 0, 1), (0, 2, 1), (2, 1, 0), (1, 0, 2)]
    table = []
    for turn in turns:
        row = []
        for node in nodes:
            corner = (node[0], node[1], 4 - node[0] - node[1])
            row.append(place[corner[turn[0]], corner[turn[1]]])
        table.append(row)
    return table


def turn_matrix():
    out = np.zeros((6 * NROWS, 128), np.float32)
    for t, row in enumerate(node_orders()):
        for n, source in enumerate(row):
            out[t * NROWS + n, source] = 1.0
    return out


def dot(a, b):
    return lax.dot_general(a, b, (((1,), (0,)), ((), ())), preferred_element_type=F32)


def halves(x):
    hi = x.astype(BF16).astype(F32)
    return hi, x - hi


def stack3(x):
    hi, lo = halves(x)
    return jnp.concatenate([hi, lo, hi, jnp.zeros((8, x.shape[1]), F32)], axis=0).astype(BF16)


def left3(a):
    hi, lo = halves(a)
    return (hi + pltpu.roll(hi, 40, 1) + pltpu.roll(lo, 80, 1)).astype(BF16)


def kernel(
    n_dev,
    dofs, cluster, neighbours, orientation, send_slots, recv_slots, jac, normals, area, bulk, invd,
    deriv, proj, turns, out,
    dofs_v, cluster_v, neigh_v, code_v, send_v, recv_v, jac_v, normal_v, area_v, bulk_v, invd_v,
    deriv_v, proj_v, turns_v,
    u_s, a_s, own_s, near_s, pad_s, fpad_s, grad_s, gradt_s, div_s, divt_s, second_s,
    trace_s, lift_s, choose_s, turn_s, pick_send, pick_local, place_recv, slot_s, zn_s, zline_s,
    zslot_s, tell_s, code_send, code_local, face_recv, coef_s,
    send0_buf, recv0_buf, send_buf, recv_buf,
    in_sem, send_sem, recv_sem,
):
    me = lax.axis_index("dom")
    steps = [k - 4 if k < 4 else k - 3 for k in range(OFFSETS)]
    partner = [lax.rem(me + (step + n_dev), n_dev) for step in steps]
    there = [me >= -step if step < 0 else me < n_dev - step for step in steps]
    barrier = pltpu.get_barrier_semaphore()
    for k in FAR_FIRST:

        @pl.when(there[k])
        def _():
            pl.semaphore_signal(
                barrier, inc=1, device_id=(partner[k],), device_id_type=pl.DeviceIdType.MESH
            )

    loads = {}

    def load(name, source, target):
        loads.setdefault(name, []).append((source, target))

    load("recv", recv_slots, recv_v)
    load("send", send_slots, send_v)
    load("code", orientation, code_v)
    load("bulk", bulk, bulk_v)
    load("invd", invd, invd_v)
    load("normal", normals, normal_v)
    load("deriv", deriv, deriv_v)
    for q in range(QUANT):
        load("dofs", dofs.at[:, q, :], dofs_v.at[q])
    load("jac", jac, jac_v)
    for f in range(4):
        load("proj", proj.at[:, f, :], proj_v.at[f])
    load("cluster", cluster, cluster_v)
    load("neigh", neighbours, neigh_v)
    load("area", area, area_v)
    load("turns", turns, turns_v)
    count = 0
    for name in loads:
        copies = []
        for source, target in loads[name]:
            copies.append(pltpu.make_async_copy(source, target, in_sem.at[count]))
            copies[-1].start()
            count += 1
        loads[name] = copies

    def ready(*names):
        for name in names:
            for copy in loads[name]:
                copy.wait()

    low = lax.broadcasted_iota(jnp.int32, (8, 128), 1) < CAP
    low1 = lax.broadcasted_iota(jnp.int32, (1, 128), 1) < CAP
    pad_s[...] = jnp.zeros_like(pad_s)
    fpad_s[...] = jnp.zeros_like(fpad_s)
    u_s[...] = jnp.zeros_like(u_s)
    slot_s[...] = jnp.zeros((16, 128), jnp.int32)

    ready("recv", "send")
    slot_s[0:8, 0:CAP] = send_v[...]
    slot_s[8:16, 0:CAP] = recv_v[...]
    both = slot_s[...]
    both = both + pltpu.roll(both, CAP, 1)

    def slot_row(first):
        tiles = [
            jnp.where(
                low1,
                both[first + 2 * p : first + 2 * p + 1],
                both[first + 2 * p + 1 : first + 2 * p + 2],
            )
            for p in TILES
        ]
        row = jnp.concatenate(tiles, axis=1)
        one, zero = jnp.ones_like(row), jnp.zeros_like(row)
        face = (
            jnp.where(row >= ELEMS, one, zero)
            + jnp.where(row >= 2 * ELEMS, one, zero)
            + jnp.where(row >= 3 * ELEMS, one, zero)
        )
        elem = jnp.where(row >= 0, row - face * ELEMS, -one)
        face = jnp.where(row >= 0, face, -one)
        return face, elem

    send_face, send_elem = slot_row(0)
    recv_face, recv_elem = slot_row(8)
    elem_rows = lax.broadcasted_iota(jnp.int32, (ELEMS, SLOTS), 0)
    pick = jnp.where(elem_rows == send_elem, 1.0, 0.0).astype(BF16)
    pick_send[0:ELEMS] = pick
    pick_send[ELEMS:] = pick

    ready("code", "bulk", "invd", "normal")
    bulk_r, invd_r = bulk_v[...], invd_v[...]
    imp = jnp.sqrt(bulk_r / invd_r)
    code = code_v[...]
    one4, zero4 = jnp.ones_like(code), jnp.zeros_like(code)
    turn_f = (
        code
        - 6 * jnp.where(code >= 6, one4, zero4)
        - 6 * jnp.where(code >= 12, one4, zero4)
        - 6 * jnp.where(code >= 18, one4, zero4)
    ).astype(F32)
    znormal = [normal_v[i] * imp for i in range(3)]
    table = []
    for f in range(4):
        zn_s[f] = jnp.zeros((8, ELEMS), F32)
        for i in range(3):
            zn_s[f, i : i + 1] = znormal[i][f : f + 1]
        zn_s[f, 3:4] = turn_f[f : f + 1]
        table.append(zn_s[f])
    table = jnp.concatenate(table, axis=0)
    t_hi, t_rest = halves(table)
    t_mid, t_lo = halves(t_rest)
    table = jnp.concatenate([t_hi, t_mid, t_lo], axis=0).astype(BF16)
    seen = dot(table, jnp.where(elem_rows == recv_elem, 1.0, 0.0).astype(BF16))
    seen = seen[0:32] + seen[32:64] + seen[64:96]
    tell = jnp.zeros((8, SLOTS), F32)
    for f in range(4):
        tell = jnp.where(recv_face == f, seen[8 * f : 8 * f + 8], tell)
    tell_s[...] = tell

    ready("deriv")
    for j in range(3):
        pad_s[j, 0:BASIS, 0:BASIS] = deriv_v[j]
    d = [pad_s[j] for j in range(3)]
    grad = jnp.concatenate([m[0:ROWS] for m in d], axis=0)
    grad_s[...] = left3(grad)

    def set_div(ref, mats):
        wide = (
            mats[0][0:ROWS]
            + pltpu.roll(mats[1][0:ROWS], 40, 1)
            + pltpu.roll(mats[2][0:ROWS], 80, 1)
        )
        hi, lo = halves(wide)
        ref[...] = jnp.concatenate([hi, hi, lo], axis=1).astype(BF16)

    set_div(div_s, d)
    products = dot(grad_s[...], jnp.concatenate([stack3(m[0:ROWS]) for m in d], axis=1))
    second = []
    for j, k in PAIRS:
        term = products[j * ROWS : (j + 1) * ROWS, k * 128 : (k + 1) * 128]
        if j != k:
            term = term + products[k * ROWS : (k + 1) * ROWS, j * 128 : (j + 1) * 128]
        second.append(term)
    second_s[...] = left3(jnp.concatenate(second, axis=0))

    ready("jac", "dofs")
    kappa = bulk_r * invd_r
    g = [[jac_v[j, i : i + 1, :] for i in range(3)] for j in range(3)]
    for j in range(3):
        for i in range(3):
            coef_s[3 * j + i : 3 * j + i + 1] = g[j][i]
            coef_s[9 + 3 * j + i : 10 + 3 * j + i] = -invd_r * g[j][i]
    for c, (j, k) in enumerate(PAIRS):
        coef_s[18 + c : 19 + c] = kappa * (
            g[j][0] * g[k][0] + g[j][1] * g[k][1] + g[j][2] * g[k][2]
        )
    for q in range(QUANT):
        u_s[q, 0:BASIS] = dofs_v[q]
    ready("proj", "cluster")
    for f in range(4):
        fpad_s[f, 0:NODES, 0:BASIS] = proj_v[f]
    faces = jnp.concatenate([fpad_s[f] for f in range(4)], axis=0)
    trace_s[...] = left3(faces)

    def coef(row):
        return coef_s[row : row + 1]

    def contra(v):
        return [
            coef(3 * j) * v[0] + coef(3 * j + 1) * v[1] + coef(3 * j + 2) * v[2] for j in range(3)
        ]

    def stack_div(w):
        parts = [halves(x) for x in w]
        pad = jnp.zeros((8, ELEMS), F32)
        his = [p[0] for p in parts] + [pad]
        los = [p[1] for p in parts] + [pad]
        return jnp.concatenate(his + los + his, axis=0).astype(BF16)

    def twice(e):
        total = coef(18) * e[0:ROWS]
        for c_at in range(1, 6):
            total = total + coef(18 + c_at) * e[c_at * ROWS : (c_at + 1) * ROWS]
        return total

    def predict(s):
        kind = cluster_v[...]
        s_vec = jnp.full(kind.shape, 0, jnp.int32) + s
        odd = jnp.bitwise_and(s_vec, 1)
        zero = jnp.zeros_like(kind)
        phase = jnp.where(kind == 0, zero, jnp.where(kind == 1, odd, s_vec))
        begin = phase.astype(F32) * STEP_LENGTH
        finish = begin + STEP_LENGTH
        b_pow, f_pow, c = begin, finish, []
        for k in range(5):
            c.append((f_pow - b_pow) * (1.0 / math.factorial(k + 1)))
            b_pow, f_pow = b_pow * begin, f_pow * finish
        left = jnp.where(
            kind == 0, zero, jnp.where(kind == 1, 1 - odd, jnp.bitwise_and(s_vec + 1, 3))
        )
        p0 = u_s[0]
        u = [u_s[i + 1] for i in range(3)]
        p1 = -bulk_v[...] * dot(div_s[...], stack_div(contra(u)))
        p2 = twice(dot(second_s[...], stack3(p0)))
        e12 = dot(second_s[...], jnp.concatenate([stack3(p1), stack3(p2)], axis=1))
        p3, p4 = twice(e12[:, 0:ELEMS]), twice(e12[:, ELEMS:])
        slope = dot(grad_s[...], stack3(c[1] * p0 + c[2] * p1 + c[3] * p2 + c[4] * p3))
        j_all = [c[0] * p0 + c[1] * p1 + c[2] * p2 + c[3] * p3 + c[4] * p4]
        for i in range(3):
            total = c[0] * u[i]
            for j in range(3):
                total = total + coef(9 + 3 * j + i) * slope[j * ROWS : (j + 1) * ROWS]
            j_all.append(total)
        return j_all, left == 0

    def two_parts(rows):
        parts = [halves(x) for x in rows]
        his = jnp.concatenate([p[0] for p in parts], axis=0)
        los = jnp.concatenate([p[1] for p in parts], axis=0)
        return jnp.concatenate([his, los], axis=1).astype(BF16)

    def chosen(parts, codes, options):
        first = jnp.zeros((8, codes.shape[1]), F32)
        second = first
        for c in range(options):
            mask = codes == c
            first = jnp.where(mask, parts[c * 16 : c * 16 + 8], first)
            second = jnp.where(mask, parts[c * 16 + 8 : c * 16 + 16], second)
        return first, second

    def packed(x0, x1):
        x1 = pltpu.roll(x1, CAP, 1)
        return jnp.where(low, x0, x1), jnp.where(low, x1, x0)

    def unpacked(even, odd):
        return pltpu.roll(jnp.where(low, odd, even), CAP, 1), jnp.where(low, even, odd)

    def first_copy(k):
        return pltpu.make_async_remote_copy(
            src_ref=send0_buf.at[k],
            dst_ref=recv0_buf.at[OFFSETS - 1 - k],
            send_sem=send_sem.at[k],
            recv_sem=recv_sem.at[0, OFFSETS - 1 - k],
            device_id=(partner[k],),
            device_id_type=pl.DeviceIdType.MESH,
        )

    def later_copy(s):
        parity = lax.rem(s, 2)

        def at(k):
            return pltpu.make_async_remote_copy(
                src_ref=send_buf.at[k],
                dst_ref=recv_buf.at[parity, OFFSETS - 1 - k],
                send_sem=send_sem.at[k],
                recv_sem=recv_sem.at[parity, OFFSETS - 1 - k],
                device_id=(partner[k],),
                device_id_type=pl.DeviceIdType.MESH,
            )

        return at

    def start(copy, rows):
        for k in rows:
            pl.when(there[k])(lambda k=k: copy(k).start())

    def finish_sends(copy):
        for k in FAR_FIRST:
            pl.when(there[k])(lambda k=k: copy(k).wait_send())

    def arrive(copy):
        for k in FAR_FIRST[::-1]:
            pl.when(there[k])(lambda k=k: copy(OFFSETS - 1 - k).wait_recv())

    def meanwhile(j_all, j_two, traced, done):
        at_face = dot(j_two, pick_local[...])
        mix = at_face[0:ROWS]
        for i in range(3):
            mix = mix - zline_s[i : i + 1] * at_face[(i + 1) * ROWS : (i + 2) * ROWS]
        first, second = chosen(dot(choose_s[...], stack3(mix)), code_local[...], 24)
        for f in range(4):
            rows = slice(f * NROWS, (f + 1) * NROWS)
            near_s[f * NROWS : f * NROWS + 8] += first[:, f * ELEMS : (f + 1) * ELEMS]
            near_s[f * NROWS + 8 : f * NROWS + 16] += second[:, f * ELEMS : (f + 1) * ELEMS]
            mine = traced[rows, 0:ELEMS]
            for i in range(3):
                mine = mine + zn_s[f, i : i + 1] * traced[rows, (i + 1) * ELEMS : (i + 2) * ELEMS]
            a_s[rows] += mine
        own = [own_s[q] + j_all[q] for q in range(QUANT)]
        change_p = bulk_v[...] * dot(divt_s[...], stack_div(contra(own[1:])))
        slope = dot(gradt_s[...], stack3(own[0]))
        change = [change_p]
        for i in range(3):
            total = coef(9 + i) * slope[0:ROWS]
            for j in range(1, 3):
                total = total + coef(9 + 3 * j + i) * slope[j * ROWS : (j + 1) * ROWS]
            change.append(-total)
        for q in range(QUANT):
            own_s[q] = jnp.where(done, 0.0, own[q])
            u_s[q] = jnp.where(done, u_s[q] + change[q], u_s[q])

    def complete(r0, r1, done):
        r0h, r0l = halves(r0)
        r1h, r1l = halves(r1)
        slot_face = face_recv[...]
        his, los = [], []
        for f in range(4):
            mask = slot_face == f
            his += [jnp.where(mask, r0h, 0.0), jnp.where(mask, r1h, 0.0)]
            los += [jnp.where(mask, r0l, 0.0), jnp.where(mask, r1l, 0.0)]
        placed = dot(jnp.concatenate(his + los, axis=0).astype(BF16), place_recv[...])
        near_all = near_s[...] + placed[0:64] + placed[64:128]
        a_all = a_s[...]
        near_s[...] = jnp.where(done, 0.0, near_all)
        a_s[...] = jnp.where(done, 0.0, a_all)
        flux = [[], [], [], []]
        for f in range(4):
            rows = slice(f * NROWS, (f + 1) * NROWS)
            own_f = a_all[rows]
            far_f = jnp.where(neigh_v[f : f + 1] == -1, own_f, near_all[rows])
            flux[0].append(coef(24 + f) * (own_f - far_f))
            plus = own_f + far_f
            for i in range(3):
                flux[i + 1].append(coef(28 + 3 * f + i) * plus)
        flux = jnp.concatenate([jnp.concatenate(rows, axis=0) for rows in flux], axis=1)
        hi, lo = halves(flux)
        lifted = dot(lift_s[...], jnp.concatenate([hi, lo, hi, lo], axis=0).astype(BF16))
        for q in range(QUANT):
            part = lifted[:, q * ELEMS : (q + 1) * ELEMS]
            u_s[q] = jnp.where(done, u_s[q] - part, u_s[q])

    def traces(j_all):
        return dot(trace_s[...], jnp.concatenate([stack3(x) for x in j_all], axis=1))

    j_all, done = predict(0)
    traced = traces(j_all)
    face_rows = two_parts([traced[:, q * ELEMS : (q + 1) * ELEMS] for q in range(QUANT)])
    for pos, p in enumerate(TILES):
        k0, k1 = 2 * p, 2 * p + 1
        cols = slice(pos * 128, (pos + 1) * 128)
        send0_buf[k0, 32:40] = tell[:, cols]
        send0_buf[k1, 32:40] = tell[:, cols]
    at_slot = dot(face_rows, pick_send[...])
    for q in range(QUANT):
        x = [jnp.zeros((8, SLOTS), F32)] * 2
        for f in range(4):
            for half in range(2):
                row = q * 64 + f * NROWS + 8 * half
                x[half] = jnp.where(send_face == f, at_slot[row : row + 8], x[half])
        for pos, p in enumerate(TILES):
            cols = slice(pos * 128, (pos + 1) * 128)
            b0, b1 = packed(x[0][:, cols], x[1][:, cols])
            send0_buf[2 * p, q * 8 : q * 8 + 8] = b0
            send0_buf[2 * p + 1, q * 8 : q * 8 + 8] = b1
    pl.semaphore_wait(barrier, sum(t.astype(jnp.int32) for t in there))
    start(first_copy, FAR_FIRST)

    ready("neigh", "area", "turns")
    for k in range(OFFSETS):

        @pl.when(jnp.logical_not(there[k]))
        def _():
            recv0_buf[k] = jnp.zeros((40, 128), F32)
            recv_buf[0, k] = jnp.zeros((8, 128), F32)
            recv_buf[1, k] = jnp.zeros((8, 128), F32)

    a_s[...] = jnp.zeros_like(a_s)
    near_s[...] = jnp.zeros_like(near_s)
    own_s[...] = jnp.zeros_like(own_s)
    elem_rows1 = lax.broadcasted_iota(jnp.int32, (ELEMS, ELEMS), 0)
    for f in range(4):
        cols = slice(f * ELEMS, (f + 1) * ELEMS)
        pick = jnp.where(elem_rows1 == neigh_v[f : f + 1], 1.0, 0.0).astype(BF16)
        pick_local[0:ELEMS, cols] = pick
        pick_local[ELEMS:, cols] = pick
        for i in range(3):
            zline_s[i : i + 1, cols] = znormal[i][f : f + 1]
        code_local[:, cols] = jnp.broadcast_to(code[f : f + 1], (8, ELEMS))
        size = area_v[f : f + 1]
        coef_s[24 + f : 25 + f] = 0.5 * size * bulk_r / imp
        for i in range(3):
            row = 28 + 3 * f + i
            coef_s[row : row + 1] = 0.5 * size * invd_r * normal_v[i, f : f + 1]
    elem_lanes = lax.broadcasted_iota(jnp.int32, (128, ELEMS), 1).astype(F32)
    recv_float = recv_elem.astype(F32)
    for p in range(4):
        column = jnp.broadcast_to(recv_float[:, p * 128 : (p + 1) * 128], (128, 128)).T
        column = jnp.concatenate([column, column], axis=1)
        place_recv[p * 128 : (p + 1) * 128] = jnp.where(column == elem_lanes, 1.0, 0.0).astype(BF16)
    face_recv[...] = jnp.broadcast_to(recv_face, (8, SLOTS))
    dt = [pad_s[j].T for j in range(3)]
    gradt_s[...] = left3(jnp.concatenate([m[0:ROWS] for m in dt], axis=0))
    set_div(divt_s, dt)
    lifts = jnp.concatenate([faces, jnp.zeros((64, 128), F32)], axis=0).T[0:ROWS]
    hi, lo = halves(lifts)
    lift_s[...] = jnp.concatenate(
        [hi + pltpu.roll(hi, 64, 1), lo + pltpu.roll(lo, 64, 1)], axis=1
    ).astype(BF16)
    turn_rows = turns_v[...]
    turn_s[...] = (turn_rows + pltpu.roll(turn_rows, NROWS, 1)).astype(BF16)
    turn_b = turn_rows.astype(BF16)
    for f in range(4):
        rows = jnp.concatenate(
            [faces[f * NROWS : (f + 1) * NROWS], jnp.zeros((112, 128), F32)], axis=0
        )
        choose_s[f * 96 : (f + 1) * 96] = dot(turn_b, left3(rows)).astype(BF16)

    meanwhile(j_all, two_parts(j_all), traced, done)
    arrive(first_copy)
    chi = []
    for q in range(QUANT):
        tiles = [
            unpacked(
                recv0_buf[2 * p, q * 8 : q * 8 + 8], recv0_buf[2 * p + 1, q * 8 : q * 8 + 8]
            )
            for p in TILES
        ]
        both = [jnp.concatenate([t[half] for t in tiles], axis=1) for half in range(2)]
        if q == 0:
            chi = both
        else:
            chi = [x - tell_s[q - 1 : q] * y for x, y in zip(chi, both)]
    for pos, p in enumerate(TILES):
        tile = jnp.where(low, recv0_buf[2 * p + 1, 32:40], recv0_buf[2 * p, 32:40])
        zslot_s[:, pos * 128 : (pos + 1) * 128] = pltpu.roll(tile, CAP, 1)
    code_send[...] = jnp.broadcast_to(send_face * 6 + zslot_s[3:4].astype(jnp.int32), (8, SLOTS))
    hi, lo = halves(jnp.concatenate(chi, axis=0))
    chi = jnp.concatenate([hi, lo, jnp.zeros((96, SLOTS), F32)], axis=0).astype(BF16)
    turn_now = jnp.broadcast_to(tell_s[3:4], (8, SLOTS)).astype(jnp.int32)
    r0, r1 = chosen(dot(turn_s[...], chi), turn_now, 6)
    complete(r0, r1, done)
    finish_sends(first_copy)

    def step(s, carry):
        j_all, done = predict(s)
        j_two = two_parts(j_all)
        copy = later_copy(s)
        for half in range(2):
            cols = slice(half * 256, (half + 1) * 256)
            at_slot = dot(j_two, pick_send[:, cols])
            mix = at_slot[0:ROWS]
            for i in range(3):
                mix = mix - zslot_s[i : i + 1, cols] * at_slot[(i + 1) * ROWS : (i + 2) * ROWS]
            first, second = chosen(dot(choose_s[...], stack3(mix)), code_send[:, cols], 24)
            rows = []
            for at in range(2):
                p = TILES[2 * half + at]
                lanes = slice(at * 128, (at + 1) * 128)
                send_buf[2 * p], send_buf[2 * p + 1] = packed(first[:, lanes], second[:, lanes])
                rows += [2 * p, 2 * p + 1]
            start(copy, [k for k in FAR_FIRST if k in rows])
        meanwhile(j_all, j_two, traces(j_all), done)
        arrive(copy)
        parity = lax.rem(s, 2)
        tiles = [unpacked(recv_buf[parity, 2 * p], recv_buf[parity, 2 * p + 1]) for p in TILES]
        r0 = jnp.concatenate([t[0] for t in tiles], axis=1)
        r1 = jnp.concatenate([t[1] for t in tiles], axis=1)
        complete(r0, r1, done)
        finish_sends(copy)
        return carry

    lax.fori_loop(1, SUBSTEPS, step, 0)
    copies = []
    for q in range(QUANT):
        dofs_v[q] = u_s[q, 0:BASIS]
        copies.append(pltpu.make_async_copy(dofs_v.at[q], out.at[:, q, :], in_sem.at[q]))
        copies[-1].start()
    for copy in copies:
        copy.wait()


def body(
    initial_dofs, cluster, neighbours, orientation, send_slots, recv_slots, inv_jacobian, normals,
    face_area, bulk_modulus, inv_density, deriv_mats, face_proj,
):
    n_dev = lax.axis_size("dom")
    hbm = pl.BlockSpec(memory_space=pltpu.HBM)

    def call(*operands):
        return pl.pallas_call(
            lambda *refs: kernel(n_dev, *refs),
            out_shape=jax.ShapeDtypeStruct((BASIS, QUANT, ELEMS), F32),
            in_specs=[hbm] * len(operands),
            out_specs=hbm,
            scratch_shapes=[
                pltpu.VMEM((QUANT, BASIS, ELEMS), F32),
                pltpu.VMEM((1, ELEMS), jnp.int32),
                pltpu.VMEM((4, ELEMS), jnp.int32),
                pltpu.VMEM((4, ELEMS), jnp.int32),
                pltpu.VMEM((OFFSETS, CAP), jnp.int32),
                pltpu.VMEM((OFFSETS, CAP), jnp.int32),
                pltpu.VMEM((3, 3, ELEMS), F32),
                pltpu.VMEM((3, 4, ELEMS), F32),
                pltpu.VMEM((4, ELEMS), F32),
                pltpu.VMEM((1, ELEMS), F32),
                pltpu.VMEM((1, ELEMS), F32),
                pltpu.VMEM((3, BASIS, BASIS), F32),
                pltpu.VMEM((4, NODES, BASIS), F32),
                pltpu.VMEM((6 * NROWS, 128), F32),
                pltpu.VMEM((QUANT, ROWS, ELEMS), F32),
                pltpu.VMEM((4 * NROWS, ELEMS), F32),
                pltpu.VMEM((QUANT, ROWS, ELEMS), F32),
                pltpu.VMEM((4 * NROWS, ELEMS), F32),
                pltpu.VMEM((3, 128, 128), F32),
                pltpu.VMEM((4, NROWS, 128), F32),
                pltpu.VMEM((3 * ROWS, 128), BF16),
                pltpu.VMEM((3 * ROWS, 128), BF16),
                pltpu.VMEM((ROWS, 384), BF16),
                pltpu.VMEM((ROWS, 384), BF16),
                pltpu.VMEM((6 * ROWS, 128), BF16),
                pltpu.VMEM((4 * NROWS, 128), BF16),
                pltpu.VMEM((ROWS, 256), BF16),
                pltpu.VMEM((24 * NROWS, 128), BF16),
                pltpu.VMEM((6 * NROWS, 128), BF16),
                pltpu.VMEM((2 * ELEMS, SLOTS), BF16),
                pltpu.VMEM((2 * ELEMS, FACES), BF16),
                pltpu.VMEM((SLOTS, ELEMS), BF16),
                pltpu.VMEM((16, 128), jnp.int32),
                pltpu.VMEM((4, 8, ELEMS), F32),
                pltpu.VMEM((8, FACES), F32),
                pltpu.VMEM((8, SLOTS), F32),
                pltpu.VMEM((8, SLOTS), F32),
                pltpu.VMEM((8, SLOTS), jnp.int32),
                pltpu.VMEM((8, FACES), jnp.int32),
                pltpu.VMEM((8, SLOTS), jnp.int32),
                pltpu.VMEM((40, ELEMS), F32),
                pltpu.VMEM((OFFSETS, 40, 128), F32),
                pltpu.VMEM((OFFSETS, 40, 128), F32),
                pltpu.VMEM((OFFSETS, 8, 128), F32),
                pltpu.VMEM((2, OFFSETS, 8, 128), F32),
                pltpu.SemaphoreType.DMA((20,)),
                pltpu.SemaphoreType.DMA((OFFSETS,)),
                pltpu.SemaphoreType.DMA((2, OFFSETS)),
            ],
            compiler_params=pltpu.CompilerParams(
                collective_id=0, has_side_effects=True, vmem_limit_bytes=64 * 1024 * 1024
            ),
        )(*operands)

    result = call(
        jnp.transpose(initial_dofs, (1, 0, 2)),
        cluster.reshape(1, ELEMS),
        neighbours,
        orientation,
        send_slots,
        recv_slots,
        inv_jacobian,
        jnp.transpose(normals, (1, 0, 2)),
        face_area,
        bulk_modulus.reshape(1, ELEMS),
        inv_density.reshape(1, ELEMS),
        deriv_mats,
        jnp.transpose(face_proj, (1, 0, 2)),
        jnp.asarray(turn_matrix()),
    )
    return jnp.transpose(result, (1, 0, 2))


def solution(mesh):
    return jax.shard_map(
        body,
        mesh=mesh,
        in_specs=(
            P(None, None, "dom"),
            P("dom"),
            P(None, "dom"),
            P(None, "dom"),
            P(None, "dom"),
            P(None, "dom"),
            P(None, None, "dom"),
            P(None, None, "dom"),
            P(None, "dom"),
            P("dom"),
            P("dom"),
            P(),
            P(),
        ),
        out_specs=P(None, None, "dom"),
        check_vma=False,
    )
```

time: 44.8 us -> 36 us (0.80)
  the two profiles are of different devices: /device:TPU:1 before, /device:TPU:25 now
where the time goes in v2:
time: 36 us; the launch traced here: 35.6 us
  Pallas kernels  34 us (94%)
  local copies, waits for them, and re-layouts  1.58 us (4%)
    pallas_call x1, Pallas kernels, call(): pl.pallas_call(lambda *refs: kernel(n_dev, *refs), out_shape=jax.ShapeDty...  34 us
    unnamed x1, local copies, waits for them, and re-layouts  1.58 us

profile of v2, /device:TPU:25, one launch (start us, length us, event | category | flops | bytes accessed | tf_op | source)
XLA Modules:
  0.0 35.6 jit_solution(304167353000281328)
XLA Ops:
  0.0 34.0 %shard_map.136 = f32[35,4,256]{2,1,0:T(4,128)} custom-call(f32[35,4,256]{2,1,0:T(4,128)} %bitcast.8, s32[1,256]{1,0:T(1,128)} %bitcast.11, s32[4,256]{1,0:T(4,128)} %refs_2_.1, s32[4,256]{1,0:T(4,128)} %refs_3_.1, s32[8,64]{1,0:T(8,128)} %refs_4_.1, s32[8,64]{1,0:T(8,128)} %refs_5_.1, f32[3,3,256]{2,1,0:T(4,128)} %refs_6_.1, f32[3,4,256]{2,1,0:T(4,128)} %bitcast.10, ...), custom_call_target="tpu_custom_call" | custom-call | tf_op jit(solution)/shard_map/pallas_call | solution.py:560
  34.0 1.6 %copy.16 = f32[4,35,256]{2,0,1:T(4,128)} copy(f32[4,35,256]{2,0,1:T(4,128)} %bitcast.7) | data formatting | bytes 286720

commit v3 on v2

--- a/solution.py
+++ b/solution.py
@@ -40,11 +40,10 @@
     return table
 
 
-def turn_matrix():
-    out = np.zeros((6 * NROWS, 128), np.float32)
+def turn_table():
+    out = np.full((NROWS, 128), NODES, np.int32)
     for t, row in enumerate(node_orders()):
-        for n, source in enumerate(row):
-            out[t * NROWS + n, source] = 1.0
+        out[:NODES, t] = row
     return out
 
 
@@ -74,9 +73,9 @@
     dofs_v, cluster_v, neigh_v, code_v, send_v, recv_v, jac_v, normal_v, area_v, bulk_v, invd_v,
     deriv_v, proj_v, turns_v,
     u_s, a_s, own_s, near_s, pad_s, fpad_s, grad_s, gradt_s, div_s, divt_s, second_s,
-    trace_s, lift_s, choose_s, turn_s, pick_send, pick_local, place_recv, slot_s, zn_s, zline_s,
-    zslot_s, tell_s, code_send, code_local, face_recv, coef_s,
-    send0_buf, recv0_buf, send_buf, recv_buf,
+    trace_s, lift_s, pick_send, pick_local, place_recv, slot_s, zn_s, zline_s,
+    zslot_s, face_send, face_local, face_recv, turn_send, turn_local, turn_recv, coef_s,
+    tell_s, send0_buf, recv0_buf, send_buf, recv_buf,
     in_sem, send_sem, recv_sem,
 ):
     me = lax.axis_index("dom")
@@ -172,12 +171,13 @@
     imp = jnp.sqrt(bulk_r / invd_r)
     code = code_v[...]
     one4, zero4 = jnp.ones_like(code), jnp.zeros_like(code)
-    turn_f = (
-        code
-        - 6 * jnp.where(code >= 6, one4, zero4)
-        - 6 * jnp.where(code >= 12, one4, zero4)
-        - 6 * jnp.where(code >= 18, one4, zero4)
-    ).astype(F32)
+    source_face = (
+        jnp.where(code >= 6, one4, zero4)
+        + jnp.where(code >= 12, one4, zero4)
+        + jnp.where(code >= 18, one4, zero4)
+    )
+    turn = code - 6 * source_face
+    turn_f = turn.astype(F32)
     znormal = [normal_v[i] * imp for i in range(3)]
     table = []
     for f in range(4):
@@ -299,14 +299,36 @@
         los = jnp.concatenate([p[1] for p in parts], axis=0)
         return jnp.concatenate([his, los], axis=1).astype(BF16)
 
-    def chosen(parts, codes, options):
-        first = jnp.zeros((8, codes.shape[1]), F32)
-        second = first
-        for c in range(options):
-            mask = codes == c
-            first = jnp.where(mask, parts[c * 16 : c * 16 + 8], first)
-            second = jnp.where(mask, parts[c * 16 + 8 : c * 16 + 16], second)
+    def chosen(parts, faces):
+        first, second = parts[0:8], parts[8:16]
+        for f in range(1, 4):
+            mask = faces == f
+            first = jnp.where(mask, parts[f * 16 : f * 16 + 8], first)
+            second = jnp.where(mask, parts[f * 16 + 8 : f * 16 + 16], second)
         return first, second
+
+    def set_turns(ref, turn_row):
+        table = turns_v[...]
+        for half in range(2):
+            rows = slice(8 * half, 8 * half + 8)
+            places = jnp.broadcast_to(table[rows, 0:1], (8, turn_row.shape[1]))
+            for t in range(1, 6):
+                places = jnp.where(turn_row == t, table[rows, t : t + 1], places)
+            ref[rows] = places
+
+    def turned(first, second, places):
+        out = []
+        for half in range(2):
+            place = places[8 * half : 8 * half + 8]
+            row = jnp.bitwise_and(place, 7)
+            out.append(
+                jnp.where(
+                    place < 8,
+                    jnp.take_along_axis(first, row, axis=0),
+                    jnp.take_along_axis(second, row, axis=0),
+                )
+            )
+        return out
 
     def packed(x0, x1):
         x1 = pltpu.roll(x1, CAP, 1)
@@ -357,7 +379,8 @@
         mix = at_face[0:ROWS]
         for i in range(3):
             mix = mix - zline_s[i : i + 1] * at_face[(i + 1) * ROWS : (i + 2) * ROWS]
-        first, second = chosen(dot(choose_s[...], stack3(mix)), code_local[...], 24)
+        first, second = chosen(dot(trace_s[...], stack3(mix)), face_local[...])
+        first, second = turned(first, second, turn_local[...])
         for f in range(4):
             rows = slice(f * NROWS, (f + 1) * NROWS)
             near_s[f * NROWS : f * NROWS + 8] += first[:, f * ELEMS : (f + 1) * ELEMS]
@@ -415,18 +438,15 @@
     j_all, done = predict(0)
     traced = traces(j_all)
     face_rows = two_parts([traced[:, q * ELEMS : (q + 1) * ELEMS] for q in range(QUANT)])
-    for pos, p in enumerate(TILES):
-        k0, k1 = 2 * p, 2 * p + 1
-        cols = slice(pos * 128, (pos + 1) * 128)
-        send0_buf[k0, 32:40] = tell[:, cols]
-        send0_buf[k1, 32:40] = tell[:, cols]
     at_slot = dot(face_rows, pick_send[...])
+    last_row = lax.broadcasted_iota(jnp.int32, (8, SLOTS), 0) == 7
     for q in range(QUANT):
         x = [jnp.zeros((8, SLOTS), F32)] * 2
         for f in range(4):
             for half in range(2):
                 row = q * 64 + f * NROWS + 8 * half
                 x[half] = jnp.where(send_face == f, at_slot[row : row + 8], x[half])
+        x[1] = jnp.where(last_row, tell[q : q + 1], x[1])
         for pos, p in enumerate(TILES):
             cols = slice(pos * 128, (pos + 1) * 128)
             b0, b1 = packed(x[0][:, cols], x[1][:, cols])
@@ -440,7 +460,7 @@
 
         @pl.when(jnp.logical_not(there[k]))
         def _():
-            recv0_buf[k] = jnp.zeros((40, 128), F32)
+            recv0_buf[k] = jnp.zeros((32, 128), F32)
             recv_buf[0, k] = jnp.zeros((8, 128), F32)
             recv_buf[1, k] = jnp.zeros((8, 128), F32)
 
@@ -455,7 +475,7 @@
         pick_local[ELEMS:, cols] = pick
         for i in range(3):
             zline_s[i : i + 1, cols] = znormal[i][f : f + 1]
-        code_local[:, cols] = jnp.broadcast_to(code[f : f + 1], (8, ELEMS))
+        face_local[:, cols] = jnp.broadcast_to(source_face[f : f + 1], (8, ELEMS))
         size = area_v[f : f + 1]
         coef_s[24 + f : 25 + f] = 0.5 * size * bulk_r / imp
         for i in range(3):
@@ -476,14 +496,9 @@
     lift_s[...] = jnp.concatenate(
         [hi + pltpu.roll(hi, 64, 1), lo + pltpu.roll(lo, 64, 1)], axis=1
     ).astype(BF16)
-    turn_rows = turns_v[...]
-    turn_s[...] = (turn_rows + pltpu.roll(turn_rows, NROWS, 1)).astype(BF16)
-    turn_b = turn_rows.astype(BF16)
-    for f in range(4):
-        rows = jnp.concatenate(
-            [faces[f * NROWS : (f + 1) * NROWS], jnp.zeros((112, 128), F32)], axis=0
-        )
-        choose_s[f * 96 : (f + 1) * 96] = dot(turn_b, left3(rows)).astype(BF16)
+    face_send[...] = jnp.broadcast_to(send_face, (8, SLOTS))
+    set_turns(turn_local, jnp.concatenate([turn[f : f + 1] for f in range(4)], axis=1))
+    set_turns(turn_recv, tell[3:4].astype(jnp.int32))
 
     meanwhile(j_all, two_parts(j_all), traced, done)
     arrive(first_copy)
@@ -496,19 +511,14 @@
             for p in TILES
         ]
         both = [jnp.concatenate([t[half] for t in tiles], axis=1) for half in range(2)]
+        zslot_s[q : q + 1] = both[1][7:8]
         if q == 0:
             chi = both
         else:
             chi = [x - tell_s[q - 1 : q] * y for x, y in zip(chi, both)]
-    for pos, p in enumerate(TILES):
-        tile = jnp.where(low, recv0_buf[2 * p + 1, 32:40], recv0_buf[2 * p, 32:40])
-        zslot_s[:, pos * 128 : (pos + 1) * 128] = pltpu.roll(tile, CAP, 1)
-    code_send[...] = jnp.broadcast_to(send_face * 6 + zslot_s[3:4].astype(jnp.int32), (8, SLOTS))
-    hi, lo = halves(jnp.concatenate(chi, axis=0))
-    chi = jnp.concatenate([hi, lo, jnp.zeros((96, SLOTS), F32)], axis=0).astype(BF16)
-    turn_now = jnp.broadcast_to(tell_s[3:4], (8, SLOTS)).astype(jnp.int32)
-    r0, r1 = chosen(dot(turn_s[...], chi), turn_now, 6)
+    r0, r1 = turned(chi[0], chi[1], turn_recv[...])
     complete(r0, r1, done)
+    set_turns(turn_send, zslot_s[3:4].astype(jnp.int32))
     finish_sends(first_copy)
 
     def step(s, carry):
@@ -521,7 +531,8 @@
             mix = at_slot[0:ROWS]
             for i in range(3):
                 mix = mix - zslot_s[i : i + 1, cols] * at_slot[(i + 1) * ROWS : (i + 2) * ROWS]
-            first, second = chosen(dot(choose_s[...], stack3(mix)), code_send[:, cols], 24)
+            first, second = chosen(dot(trace_s[...], stack3(mix)), face_send[:, cols])
+            first, second = turned(first, second, turn_send[:, cols])
             rows = []
             for at in range(2):
                 p = TILES[2 * half + at]
@@ -576,7 +587,7 @@
                 pltpu.VMEM((1, ELEMS), F32),
                 pltpu.VMEM((3, BASIS, BASIS), F32),
                 pltpu.VMEM((4, NODES, BASIS), F32),
-                pltpu.VMEM((6 * NROWS, 128), F32),
+                pltpu.VMEM((NROWS, 128), jnp.int32),
                 pltpu.VMEM((QUANT, ROWS, ELEMS), F32),
                 pltpu.VMEM((4 * NROWS, ELEMS), F32),
                 pltpu.VMEM((QUANT, ROWS, ELEMS), F32),
@@ -590,8 +601,6 @@
                 pltpu.VMEM((6 * ROWS, 128), BF16),
                 pltpu.VMEM((4 * NROWS, 128), BF16),
                 pltpu.VMEM((ROWS, 256), BF16),
-                pltpu.VMEM((24 * NROWS, 128), BF16),
-                pltpu.VMEM((6 * NROWS, 128), BF16),
                 pltpu.VMEM((2 * ELEMS, SLOTS), BF16),
                 pltpu.VMEM((2 * ELEMS, FACES), BF16),
                 pltpu.VMEM((SLOTS, ELEMS), BF16),
@@ -599,13 +608,16 @@
                 pltpu.VMEM((4, 8, ELEMS), F32),
                 pltpu.VMEM((8, FACES), F32),
                 pltpu.VMEM((8, SLOTS), F32),
-                pltpu.VMEM((8, SLOTS), F32),
                 pltpu.VMEM((8, SLOTS), jnp.int32),
                 pltpu.VMEM((8, FACES), jnp.int32),
                 pltpu.VMEM((8, SLOTS), jnp.int32),
+                pltpu.VMEM((NROWS, SLOTS), jnp.int32),
+                pltpu.VMEM((NROWS, FACES), jnp.int32),
+                pltpu.VMEM((NROWS, SLOTS), jnp.int32),
                 pltpu.VMEM((40, ELEMS), F32),
-                pltpu.VMEM((OFFSETS, 40, 128), F32),
-                pltpu.VMEM((OFFSETS, 40, 128), F32),
+                pltpu.VMEM((8, SLOTS), F32),
+                pltpu.VMEM((OFFSETS, 32, 128), F32),
+                pltpu.VMEM((OFFSETS, 32, 128), F32),
                 pltpu.VMEM((OFFSETS, 8, 128), F32),
                 pltpu.VMEM((2, OFFSETS, 8, 128), F32),
                 pltpu.SemaphoreType.DMA((20,)),
@@ -631,7 +643,7 @@
         inv_density.reshape(1, ELEMS),
         deriv_mats,
         jnp.transpose(face_proj, (1, 0, 2)),
-        jnp.asarray(turn_matrix()),
+        jnp.asarray(turn_table()),
     )
     return jnp.transpose(result, (1, 0, 2))
 

time: 36 us -> 35.1 us (0.975)
  Pallas kernels: 34 us -> 33.1 us
    pallas_call x1, Pallas kernels: 34 us -> 33.1 us  [call(): pl.pallas_call(lambda *refs: kernel(n_dev, *refs), out_shape=jax.ShapeDty...]
where the time goes in v3:
time: 35.1 us; the launch traced here: 34.7 us
  Pallas kernels  33.1 us (94%)
  local copies, waits for them, and re-layouts  1.58 us (5%)
    pallas_call x1, Pallas kernels, call(): pl.pallas_call(lambda *refs: kernel(n_dev, *refs), out_shape=jax.ShapeDty...  33.1 us
    unnamed x1, local copies, waits for them, and re-layouts  1.58 us

profile of v3, /device:TPU:25, one launch (start us, length us, event | category | flops | bytes accessed | tf_op | source)
XLA Modules:
  0.0 34.7 jit_solution(10291929312958568932)
XLA Ops:
  0.0 33.1 %shard_map.136 = f32[35,4,256]{2,1,0:T(4,128)} custom-call(f32[35,4,256]{2,1,0:T(4,128)} %bitcast.8, s32[1,256]{1,0:T(1,128)} %bitcast.11, s32[4,256]{1,0:T(4,128)} %refs_2_.1, s32[4,256]{1,0:T(4,128)} %refs_3_.1, s32[8,64]{1,0:T(8,128)} %refs_4_.1, s32[8,64]{1,0:T(8,128)} %refs_5_.1, f32[3,3,256]{2,1,0:T(4,128)} %refs_6_.1, f32[3,4,256]{2,1,0:T(4,128)} %bitcast.10, ...), custom_call_target="tpu_custom_call" | custom-call | tf_op jit(solution)/shard_map/pallas_call | solution.py:571
  33.1 1.6 %copy.16 = f32[4,35,256]{2,0,1:T(4,128)} copy(f32[4,35,256]{2,0,1:T(4,128)} %bitcast.7) | data formatting | bytes 286720

commit v4 on v3

--- a/solution.py
+++ b/solution.py
@@ -10,6 +10,7 @@
 
 SUBSTEPS = 4
 STEP_LENGTH = 0.3
+VMEM_BYTES = 55112 * 1024
 QUANT = 4
 BASIS = 35
 ROWS = 40
@@ -73,7 +74,7 @@
     dofs_v, cluster_v, neigh_v, code_v, send_v, recv_v, jac_v, normal_v, area_v, bulk_v, invd_v,
     deriv_v, proj_v, turns_v,
     u_s, a_s, own_s, near_s, pad_s, fpad_s, grad_s, gradt_s, div_s, divt_s, second_s,
-    trace_s, lift_s, pick_send, pick_local, place_recv, slot_s, zn_s, zline_s,
+    trace_s, lift_s, flux1_s, flux2_s, p_s, pick_send, pick_local, place_recv, slot_s, zn_s, zline_s,
     zslot_s, face_send, face_local, face_recv, turn_send, turn_local, turn_recv, coef_s,
     tell_s, send0_buf, recv0_buf, send_buf, recv_buf,
     in_sem, send_sem, recv_sem,
@@ -278,10 +279,8 @@
         left = jnp.where(
             kind == 0, zero, jnp.where(kind == 1, 1 - odd, jnp.bitwise_and(s_vec + 1, 3))
         )
-        p0 = u_s[0]
+        p0, p1, p2 = u_s[0], p_s[0], p_s[1]
         u = [u_s[i + 1] for i in range(3)]
-        p1 = -bulk_v[...] * dot(div_s[...], stack_div(contra(u)))
-        p2 = twice(dot(second_s[...], stack3(p0)))
         e12 = dot(second_s[...], jnp.concatenate([stack3(p1), stack3(p2)], axis=1))
         p3, p4 = twice(e12[:, 0:ELEMS]), twice(e12[:, ELEMS:])
         slope = dot(grad_s[...], stack3(c[1] * p0 + c[2] * p1 + c[3] * p2 + c[4] * p3))
@@ -292,6 +291,10 @@
                 total = total + coef(9 + 3 * j + i) * slope[j * ROWS : (j + 1) * ROWS]
             j_all.append(total)
         return j_all, left == 0
+
+    def first_terms():
+        p_s[0] = -bulk_v[...] * dot(div_s[...], stack_div(contra([u_s[i + 1] for i in range(3)])))
+        p_s[1] = twice(dot(second_s[...], stack3(u_s[0])))
 
     def two_parts(rows):
         parts = [halves(x) for x in rows]
@@ -401,6 +404,7 @@
         for q in range(QUANT):
             own_s[q] = jnp.where(done, 0.0, own[q])
             u_s[q] = jnp.where(done, u_s[q] + change[q], u_s[q])
+        first_terms()
 
     def complete(r0, r1, done):
         r0h, r0l = halves(r0)
@@ -416,7 +420,7 @@
         a_all = a_s[...]
         near_s[...] = jnp.where(done, 0.0, near_all)
         a_s[...] = jnp.where(done, 0.0, a_all)
-        flux = [[], [], [], []]
+        flux, slopes = [[], [], [], []], [[], [], []]
         for f in range(4):
             rows = slice(f * NROWS, (f + 1) * NROWS)
             own_f = a_all[rows]
@@ -425,9 +429,18 @@
             plus = own_f + far_f
             for i in range(3):
                 flux[i + 1].append(coef(28 + 3 * f + i) * plus)
+                slopes[i].append(coef(40 + 3 * f + i) * plus)
         flux = jnp.concatenate([jnp.concatenate(rows, axis=0) for rows in flux], axis=1)
         hi, lo = halves(flux)
-        lifted = dot(lift_s[...], jnp.concatenate([hi, lo, hi, lo], axis=0).astype(BF16))
+        flux = jnp.concatenate([hi, lo, hi, lo], axis=0).astype(BF16)
+        hi, lo = halves(jnp.concatenate([x for rows in slopes for x in rows], axis=0))
+        pad = jnp.zeros((64, ELEMS), F32)
+        slopes = jnp.concatenate([hi, pad, lo, pad, hi, pad], axis=0).astype(BF16)
+        change_1 = bulk_v[...] * dot(flux1_s[...], slopes)
+        change_2 = twice(dot(flux2_s[...], flux[:, 0:ELEMS]))
+        p_s[0] = jnp.where(done, p_s[0] + change_1, p_s[0])
+        p_s[1] = jnp.where(done, p_s[1] - change_2, p_s[1])
+        lifted = dot(lift_s[...], flux)
         for q in range(QUANT):
             part = lifted[:, q * ELEMS : (q + 1) * ELEMS]
             u_s[q] = jnp.where(done, u_s[q] - part, u_s[q])
@@ -435,6 +448,7 @@
     def traces(j_all):
         return dot(trace_s[...], jnp.concatenate([stack3(x) for x in j_all], axis=1))
 
+    first_terms()
     j_all, done = predict(0)
     traced = traces(j_all)
     face_rows = two_parts([traced[:, q * ELEMS : (q + 1) * ELEMS] for q in range(QUANT)])
@@ -481,6 +495,13 @@
         for i in range(3):
             row = 28 + 3 * f + i
             coef_s[row : row + 1] = 0.5 * size * invd_r * normal_v[i, f : f + 1]
+        for j in range(3):
+            row = 40 + 3 * f + j
+            coef_s[row : row + 1] = (0.5 * size * invd_r) * (
+                g[j][0] * normal_v[0, f : f + 1]
+                + g[j][1] * normal_v[1, f : f + 1]
+                + g[j][2] * normal_v[2, f : f + 1]
+            )
     elem_lanes = lax.broadcasted_iota(jnp.int32, (128, ELEMS), 1).astype(F32)
     recv_float = recv_elem.astype(F32)
     for p in range(4):
@@ -492,10 +513,22 @@
     gradt_s[...] = left3(jnp.concatenate([m[0:ROWS] for m in dt], axis=0))
     set_div(divt_s, dt)
     lifts = jnp.concatenate([faces, jnp.zeros((64, 128), F32)], axis=0).T[0:ROWS]
-    hi, lo = halves(lifts)
-    lift_s[...] = jnp.concatenate(
-        [hi + pltpu.roll(hi, 64, 1), lo + pltpu.roll(lo, 64, 1)], axis=1
-    ).astype(BF16)
+
+    def left4(a):
+        hi, lo = halves(a)
+        return jnp.concatenate(
+            [hi + pltpu.roll(hi, 64, 1), lo + pltpu.roll(lo, 64, 1)], axis=1
+        ).astype(BF16)
+
+    lift_s[...] = left4(lifts)
+    lifts = stack3(lifts)
+    flux2_s[...] = left4(dot(second_s[...], lifts))
+    slope = dot(grad_s[...], lifts)
+    wide = jnp.concatenate(
+        [slope[0:ROWS] + pltpu.roll(slope[ROWS : 2 * ROWS], 64, 1), slope[2 * ROWS :]], axis=1
+    )
+    hi, lo = halves(wide)
+    flux1_s[...] = jnp.concatenate([hi, hi, lo], axis=1).astype(BF16)
     face_send[...] = jnp.broadcast_to(send_face, (8, SLOTS))
     set_turns(turn_local, jnp.concatenate([turn[f : f + 1] for f in range(4)], axis=1))
     set_turns(turn_recv, tell[3:4].astype(jnp.int32))
@@ -551,13 +584,8 @@
         return carry
 
     lax.fori_loop(1, SUBSTEPS, step, 0)
-    copies = []
     for q in range(QUANT):
-        dofs_v[q] = u_s[q, 0:BASIS]
-        copies.append(pltpu.make_async_copy(dofs_v.at[q], out.at[:, q, :], in_sem.at[q]))
-        copies[-1].start()
-    for copy in copies:
-        copy.wait()
+        out[q] = u_s[q, 0:BASIS]
 
 
 def body(
@@ -570,9 +598,9 @@
     def call(*operands):
         return pl.pallas_call(
             lambda *refs: kernel(n_dev, *refs),
-            out_shape=jax.ShapeDtypeStruct((BASIS, QUANT, ELEMS), F32),
+            out_shape=pltpu.VMEM((QUANT, BASIS, ELEMS), F32),
             in_specs=[hbm] * len(operands),
-            out_specs=hbm,
+            out_specs=pl.BlockSpec(memory_space=pltpu.VMEM),
             scratch_shapes=[
                 pltpu.VMEM((QUANT, BASIS, ELEMS), F32),
                 pltpu.VMEM((1, ELEMS), jnp.int32),
@@ -601,6 +629,9 @@
                 pltpu.VMEM((6 * ROWS, 128), BF16),
                 pltpu.VMEM((4 * NROWS, 128), BF16),
                 pltpu.VMEM((ROWS, 256), BF16),
+                pltpu.VMEM((ROWS, 768), BF16),
+                pltpu.VMEM((6 * ROWS, 256), BF16),
+                pltpu.VMEM((2, ROWS, ELEMS), F32),
                 pltpu.VMEM((2 * ELEMS, SLOTS), BF16),
                 pltpu.VMEM((2 * ELEMS, FACES), BF16),
                 pltpu.VMEM((SLOTS, ELEMS), BF16),
@@ -614,7 +645,7 @@
                 pltpu.VMEM((NROWS, SLOTS), jnp.int32),
                 pltpu.VMEM((NROWS, FACES), jnp.int32),
                 pltpu.VMEM((NROWS, SLOTS), jnp.int32),
-                pltpu.VMEM((40, ELEMS), F32),
+                pltpu.VMEM((56, ELEMS), F32),
                 pltpu.VMEM((8, SLOTS), F32),
                 pltpu.VMEM((OFFSETS, 32, 128), F32),
                 pltpu.VMEM((OFFSETS, 32, 128), F32),
@@ -625,7 +656,7 @@
                 pltpu.SemaphoreType.DMA((2, OFFSETS)),
             ],
             compiler_params=pltpu.CompilerParams(
-                collective_id=0, has_side_effects=True, vmem_limit_bytes=64 * 1024 * 1024
+                collective_id=0, has_side_effects=True, vmem_limit_bytes=VMEM_BYTES
             ),
         )(*operands)
 
@@ -645,7 +676,7 @@
         jnp.transpose(face_proj, (1, 0, 2)),
         jnp.asarray(turn_table()),
     )
-    return jnp.transpose(result, (1, 0, 2))
+    return result
 
 
 def solution(mesh):

time: 35.1 us -> 33.2 us (0.946)
  Pallas kernels: 33.1 us -> 32 us
  local copies, waits for them, and re-layouts: 1.58 us -> 0.72 us
    unnamed x1 -> x0, local copies, waits for them, and re-layouts: 1.58 us -> none
    pallas_call x1, Pallas kernels: 33.1 us -> 32 us  [call(): pl.pallas_call(lambda *refs: kernel(n_dev, *refs), out_shape=pltpu.VMEM((...]
    pallas_call x0 -> x1, local copies, waits for them, and re-layouts: none -> 0.72 us  [call(): pl.pallas_call(lambda *refs: kernel(n_dev, *refs), out_shape=pltpu.VMEM((...]
where the time goes in v4:
time: 33.2 us; the launch traced here: 32.8 us
  Pallas kernels  32 us (96%)
  local copies, waits for them, and re-layouts  0.72 us (2%)
    pallas_call x1, Pallas kernels, call(): pl.pallas_call(lambda *refs: kernel(n_dev, *refs), out_shape=pltpu.VMEM((...  32 us
    pallas_call x1, local copies, waits for them, and re-layouts, call(): pl.pallas_call(lambda *refs: kernel(n_dev, *refs), out_shape=pltpu.VMEM((...  0.72 us

profile of v4, /device:TPU:25, one launch (start us, length us, event | category | flops | bytes accessed | tf_op | source)
XLA Modules:
  0.0 32.8 jit_solution(15114970777272696570)
XLA Ops:
  0.0 32.0 %shard_map.136 = f32[4,35,256]{2,1,0:T(8,128)S(1)} custom-call(f32[35,4,256]{2,1,0:T(4,128)} %bitcast.6, s32[1,256]{1,0:T(1,128)} %bitcast.9, s32[4,256]{1,0:T(4,128)} %refs_2_.1, s32[4,256]{1,0:T(4,128)} %refs_3_.1, s32[8,64]{1,0:T(8,128)} %refs_4_.1, s32[8,64]{1,0:T(8,128)} %refs_5_.1, f32[3,3,256]{2,1,0:T(4,128)} %refs_6_.1, f32[3,4,256]{2,1,0:T(4,128)} %bitcast.8, ...), custom_call_target="tpu_custom_call" | custom-call | tf_op jit(solution)/shard_map/pallas_call | solution.py:599
  32.1 0.7 %copy.15 = f32[4,35,256]{2,0,1:T(4,128)} copy(f32[4,35,256]{2,1,0:T(8,128)S(1)} %shard_map.136) | data formatting | bytes 286720 | tf_op jit(solution)/shard_map/pallas_call | solution.py:599

commit v5 on v4

--- a/solution.py
+++ b/solution.py
@@ -74,7 +74,7 @@
     dofs_v, cluster_v, neigh_v, code_v, send_v, recv_v, jac_v, normal_v, area_v, bulk_v, invd_v,
     deriv_v, proj_v, turns_v,
     u_s, a_s, own_s, near_s, pad_s, fpad_s, grad_s, gradt_s, div_s, divt_s, second_s,
-    trace_s, lift_s, flux1_s, flux2_s, p_s, pick_send, pick_local, place_recv, slot_s, zn_s, zline_s,
+    trace_s, lift_s, flux1_s, flux2_s, p_s, j_s, wide_s, gslot_s, yslot_s, pick_send, pick_local, place_recv, slot_s, zn_s, zline_s,
     zslot_s, face_send, face_local, face_recv, turn_send, turn_local, turn_recv, coef_s,
     tell_s, send0_buf, recv0_buf, send_buf, recv_buf,
     in_sem, send_sem, recv_sem,
@@ -264,33 +264,52 @@
             total = total + coef(18 + c_at) * e[c_at * ROWS : (c_at + 1) * ROWS]
         return total
 
-    def predict(s):
+    def weights(s):
         kind = cluster_v[...]
         s_vec = jnp.full(kind.shape, 0, jnp.int32) + s
-        odd = jnp.bitwise_and(s_vec, 1)
-        zero = jnp.zeros_like(kind)
-        phase = jnp.where(kind == 0, zero, jnp.where(kind == 1, odd, s_vec))
+        phase = jnp.where(
+            kind == 0,
+            jnp.zeros_like(kind),
+            jnp.where(kind == 1, jnp.bitwise_and(s_vec, 1), s_vec),
+        )
         begin = phase.astype(F32) * STEP_LENGTH
         finish = begin + STEP_LENGTH
         b_pow, f_pow, c = begin, finish, []
         for k in range(5):
             c.append((f_pow - b_pow) * (1.0 / math.factorial(k + 1)))
             b_pow, f_pow = b_pow * begin, f_pow * finish
-        left = jnp.where(
-            kind == 0, zero, jnp.where(kind == 1, 1 - odd, jnp.bitwise_and(s_vec + 1, 3))
-        )
+        return c
+
+    def series(s):
+        c = weights(s)
         p0, p1, p2 = u_s[0], p_s[0], p_s[1]
-        u = [u_s[i + 1] for i in range(3)]
         e12 = dot(second_s[...], jnp.concatenate([stack3(p1), stack3(p2)], axis=1))
         p3, p4 = twice(e12[:, 0:ELEMS]), twice(e12[:, ELEMS:])
-        slope = dot(grad_s[...], stack3(c[1] * p0 + c[2] * p1 + c[3] * p2 + c[4] * p3))
-        j_all = [c[0] * p0 + c[1] * p1 + c[2] * p2 + c[3] * p3 + c[4] * p4]
+        slope_of = c[1] * p0 + c[2] * p1 + c[3] * p2 + c[4] * p3
+        pressure = c[0] * p0 + c[1] * p1 + c[2] * p2 + c[3] * p3 + c[4] * p4
+        return pressure, slope_of, [c[0] * u_s[i + 1] for i in range(3)]
+
+    def velocities(slope_of, start_u):
+        slope = dot(grad_s[...], stack3(slope_of))
+        out = []
         for i in range(3):
-            total = c[0] * u[i]
+            total = start_u[i]
             for j in range(3):
                 total = total + coef(9 + 3 * j + i) * slope[j * ROWS : (j + 1) * ROWS]
-            j_all.append(total)
-        return j_all, left == 0
+            out.append(total)
+        return out
+
+    def ending(s):
+        kind = cluster_v[...]
+        s_vec = jnp.full(kind.shape, 0, jnp.int32) + s
+        left = jnp.where(
+            kind == 0,
+            jnp.zeros_like(kind),
+            jnp.where(
+                kind == 1, 1 - jnp.bitwise_and(s_vec, 1), jnp.bitwise_and(s_vec + 1, 3)
+            ),
+        )
+        return left == 0
 
     def first_terms():
         p_s[0] = -bulk_v[...] * dot(div_s[...], stack_div(contra([u_s[i + 1] for i in range(3)])))
@@ -373,25 +392,34 @@
         for k in FAR_FIRST:
             pl.when(there[k])(lambda k=k: copy(k).wait_send())
 
-    def arrive(copy):
+    def arrive(copy, rows):
         for k in FAR_FIRST[::-1]:
-            pl.when(there[k])(lambda k=k: copy(OFFSETS - 1 - k).wait_recv())
-
-    def meanwhile(j_all, j_two, traced, done):
+            if k in rows:
+                pl.when(there[k])(lambda k=k: copy(OFFSETS - 1 - k).wait_recv())
+
+    def meanwhile(j_all, j_two, traced, done, last=False):
         at_face = dot(j_two, pick_local[...])
         mix = at_face[0:ROWS]
         for i in range(3):
             mix = mix - zline_s[i : i + 1] * at_face[(i + 1) * ROWS : (i + 2) * ROWS]
         first, second = chosen(dot(trace_s[...], stack3(mix)), face_local[...])
         first, second = turned(first, second, turn_local[...])
+        flux = [[], [], [], []]
         for f in range(4):
             rows = slice(f * NROWS, (f + 1) * NROWS)
-            near_s[f * NROWS : f * NROWS + 8] += first[:, f * ELEMS : (f + 1) * ELEMS]
-            near_s[f * NROWS + 8 : f * NROWS + 16] += second[:, f * ELEMS : (f + 1) * ELEMS]
-            mine = traced[rows, 0:ELEMS]
+            cols = slice(f * ELEMS, (f + 1) * ELEMS)
+            near = near_s[rows] + jnp.concatenate([first[:, cols], second[:, cols]], axis=0)
+            near_s[rows] = near
+            mine = a_s[rows] + traced[rows, 0:ELEMS]
             for i in range(3):
                 mine = mine + zn_s[f, i : i + 1] * traced[rows, (i + 1) * ELEMS : (i + 2) * ELEMS]
-            a_s[rows] += mine
+            a_s[rows] = jnp.where(done, 0.0, mine)
+            far = jnp.where(neigh_v[f : f + 1] == -1, mine, near)
+            flux[0].append(coef(24 + f) * (mine - far))
+            plus = mine + far
+            for i in range(3):
+                flux[i + 1].append(coef(28 + 3 * f + i) * plus)
+        lifted = dot(lift_s[...], stack4(flux))
         own = [own_s[q] + j_all[q] for q in range(QUANT)]
         change_p = bulk_v[...] * dot(divt_s[...], stack_div(contra(own[1:])))
         slope = dot(gradt_s[...], stack3(own[0]))
@@ -403,36 +431,29 @@
             change.append(-total)
         for q in range(QUANT):
             own_s[q] = jnp.where(done, 0.0, own[q])
-            u_s[q] = jnp.where(done, u_s[q] + change[q], u_s[q])
-        first_terms()
-
-    def complete(r0, r1, done):
+            part = lifted[:, q * ELEMS : (q + 1) * ELEMS]
+            u_s[q] = jnp.where(done, u_s[q] + (change[q] - part), u_s[q])
+        if not last:
+            first_terms()
+
+    def stack4(flux):
+        flux = jnp.concatenate([jnp.concatenate(rows, axis=0) for rows in flux], axis=1)
+        hi, lo = halves(flux)
+        return jnp.concatenate([hi, lo, hi, lo], axis=0).astype(BF16)
+
+    def placed(r0, r1, cols):
         r0h, r0l = halves(r0)
         r1h, r1l = halves(r1)
-        slot_face = face_recv[...]
+        slot_face = face_recv[:, cols]
         his, los = [], []
         for f in range(4):
             mask = slot_face == f
             his += [jnp.where(mask, r0h, 0.0), jnp.where(mask, r1h, 0.0)]
             los += [jnp.where(mask, r0l, 0.0), jnp.where(mask, r1l, 0.0)]
-        placed = dot(jnp.concatenate(his + los, axis=0).astype(BF16), place_recv[...])
-        near_all = near_s[...] + placed[0:64] + placed[64:128]
-        a_all = a_s[...]
-        near_s[...] = jnp.where(done, 0.0, near_all)
-        a_s[...] = jnp.where(done, 0.0, a_all)
-        flux, slopes = [[], [], [], []], [[], [], []]
-        for f in range(4):
-            rows = slice(f * NROWS, (f + 1) * NROWS)
-            own_f = a_all[rows]
-            far_f = jnp.where(neigh_v[f : f + 1] == -1, own_f, near_all[rows])
-            flux[0].append(coef(24 + f) * (own_f - far_f))
-            plus = own_f + far_f
-            for i in range(3):
-                flux[i + 1].append(coef(28 + 3 * f + i) * plus)
-                slopes[i].append(coef(40 + 3 * f + i) * plus)
-        flux = jnp.concatenate([jnp.concatenate(rows, axis=0) for rows in flux], axis=1)
-        hi, lo = halves(flux)
-        flux = jnp.concatenate([hi, lo, hi, lo], axis=0).astype(BF16)
+        both = dot(jnp.concatenate(his + los, axis=0).astype(BF16), place_recv[cols])
+        return both[0:64] + both[64:128]
+
+    def next_terms(flux, slopes, done):
         hi, lo = halves(jnp.concatenate([x for rows in slopes for x in rows], axis=0))
         pad = jnp.zeros((64, ELEMS), F32)
         slopes = jnp.concatenate([hi, pad, lo, pad, hi, pad], axis=0).astype(BF16)
@@ -440,6 +461,19 @@
         change_2 = twice(dot(flux2_s[...], flux[:, 0:ELEMS]))
         p_s[0] = jnp.where(done, p_s[0] + change_1, p_s[0])
         p_s[1] = jnp.where(done, p_s[1] - change_2, p_s[1])
+
+    def complete(chi, done, last=False):
+        near_s[...] = jnp.where(done, 0.0, near_s[...] + chi)
+        flux, slopes = [[], [], [], []], [[], [], []]
+        for f in range(4):
+            part = chi[f * NROWS : (f + 1) * NROWS]
+            flux[0].append(-coef(24 + f) * part)
+            for i in range(3):
+                flux[i + 1].append(coef(28 + 3 * f + i) * part)
+                slopes[i].append(coef(40 + 3 * f + i) * part)
+        flux = stack4(flux)
+        if not last:
+            next_terms(flux, slopes, done)
         lifted = dot(lift_s[...], flux)
         for q in range(QUANT):
             part = lifted[:, q * ELEMS : (q + 1) * ELEMS]
@@ -449,7 +483,8 @@
         return dot(trace_s[...], jnp.concatenate([stack3(x) for x in j_all], axis=1))
 
     first_terms()
-    j_all, done = predict(0)
+    pressure, slope_of, start_u = series(0)
+    j_all, done = [pressure] + velocities(slope_of, start_u), ending(0)
     traced = traces(j_all)
     face_rows = two_parts([traced[:, q * ELEMS : (q + 1) * ELEMS] for q in range(QUANT)])
     at_slot = dot(face_rows, pick_send[...])
@@ -521,6 +556,17 @@
         ).astype(BF16)
 
     lift_s[...] = left4(lifts)
+    slope = dot(trace_s[...], jnp.concatenate([stack3(m[0:ROWS]) for m in d], axis=1))
+    wide_s[:, 0:128] = trace_s[...]
+    for j in range(3):
+        wide_s[:, (j + 1) * 128 : (j + 2) * 128] = left3(slope[:, j * 128 : (j + 1) * 128])
+    table = jnp.concatenate([coef_s[9:18], jnp.zeros((7, ELEMS), F32)], axis=0)
+    t_hi, t_rest = halves(table)
+    t_mid, t_lo = halves(t_rest)
+    seen = dot(
+        jnp.concatenate([t_hi, t_mid, t_lo], axis=0).astype(BF16), pick_send[0:ELEMS]
+    )
+    gslot_s[...] = seen[0:16] + seen[16:32] + seen[32:48]
     lifts = stack3(lifts)
     flux2_s[...] = left4(dot(second_s[...], lifts))
     slope = dot(grad_s[...], lifts)
@@ -534,56 +580,77 @@
     set_turns(turn_recv, tell[3:4].astype(jnp.int32))
 
     meanwhile(j_all, two_parts(j_all), traced, done)
-    arrive(first_copy)
-    chi = []
-    for q in range(QUANT):
-        tiles = [
-            unpacked(
-                recv0_buf[2 * p, q * 8 : q * 8 + 8], recv0_buf[2 * p + 1, q * 8 : q * 8 + 8]
-            )
-            for p in TILES
-        ]
-        both = [jnp.concatenate([t[half] for t in tiles], axis=1) for half in range(2)]
-        zslot_s[q : q + 1] = both[1][7:8]
-        if q == 0:
-            chi = both
-        else:
-            chi = [x - tell_s[q - 1 : q] * y for x, y in zip(chi, both)]
-    r0, r1 = turned(chi[0], chi[1], turn_recv[...])
-    complete(r0, r1, done)
+    finish_sends(first_copy)
+    total = None
+    for half in (1, 0):
+        pair = TILES[2 * half : 2 * half + 2]
+        cols = slice(half * 256, (half + 1) * 256)
+        arrive(first_copy, [2 * p + at for p in pair for at in range(2)])
+        for q in range(QUANT):
+            rows = slice(q * 8, q * 8 + 8)
+            tiles = [unpacked(recv0_buf[2 * p, rows], recv0_buf[2 * p + 1, rows]) for p in pair]
+            both = [jnp.concatenate([t[at] for t in tiles], axis=1) for at in range(2)]
+            zslot_s[q : q + 1, cols] = both[1][7:8]
+            if q == 0:
+                chi = both
+            else:
+                chi = [x - tell_s[q - 1 : q, cols] * y for x, y in zip(chi, both)]
+        r0, r1 = turned(chi[0], chi[1], turn_recv[:, cols])
+        part = placed(r0, r1, cols)
+        total = part if total is None else total + part
+    complete(total, done)
     set_turns(turn_send, zslot_s[3:4].astype(jnp.int32))
-    finish_sends(first_copy)
+    for j in range(3):
+        total = zslot_s[0:1] * gslot_s[3 * j : 3 * j + 1]
+        for i in range(1, 3):
+            total = total + zslot_s[i : i + 1] * gslot_s[3 * j + i : 3 * j + i + 1]
+        yslot_s[j : j + 1] = -total
+
+    def advance(s):
+        pressure, slope_of, start_u = series(s)
+        j_s[0], j_s[1] = pressure, slope_of
+        five = two_parts([pressure] + start_u + [slope_of, jnp.zeros((8, ELEMS), F32)])
+        copy = later_copy(s)
+        at_slot = dot(five, pick_send[...])
+        mix = at_slot[0:ROWS]
+        for i in range(3):
+            mix = mix - zslot_s[i : i + 1] * at_slot[(i + 1) * ROWS : (i + 2) * ROWS]
+        steep = at_slot[4 * ROWS : 5 * ROWS]
+        mix = [stack3(mix)] + [stack3(yslot_s[j : j + 1] * steep) for j in range(3)]
+        first, second = chosen(dot(wide_s[...], jnp.concatenate(mix, axis=0)), face_send[...])
+        first, second = turned(first, second, turn_send[...])
+        for pos, p in enumerate(TILES):
+            lanes = slice(pos * 128, (pos + 1) * 128)
+            send_buf[2 * p], send_buf[2 * p + 1] = packed(first[:, lanes], second[:, lanes])
+        start(copy, FAR_FIRST)
+
+    def finish(s, last=False):
+        copy, done = later_copy(s), ending(s)
+        c = weights(s)
+        j_all = [j_s[0]] + velocities(j_s[1], [c[0] * u_s[i + 1] for i in range(3)])
+        meanwhile(j_all, two_parts(j_all), traces(j_all), done, last)
+        finish_sends(copy)
+        parity = lax.rem(s, 2)
+        total = None
+        for half in (1, 0):
+            pair = TILES[2 * half : 2 * half + 2]
+            cols = slice(half * 256, (half + 1) * 256)
+            arrive(copy, [2 * p + at for p in pair for at in range(2)])
+            tiles = [unpacked(recv_buf[parity, 2 * p], recv_buf[parity, 2 * p + 1]) for p in pair]
+            r0 = jnp.concatenate([t[0] for t in tiles], axis=1)
+            r1 = jnp.concatenate([t[1] for t in tiles], axis=1)
+            part = placed(r0, r1, cols)
+            total = part if total is None else total + part
+        complete(total, done, last)
 
     def step(s, carry):
-        j_all, done = predict(s)
-        j_two = two_parts(j_all)
-        copy = later_copy(s)
-        for half in range(2):
-            cols = slice(half * 256, (half + 1) * 256)
-            at_slot = dot(j_two, pick_send[:, cols])
-            mix = at_slot[0:ROWS]
-            for i in range(3):
-                mix = mix - zslot_s[i : i + 1, cols] * at_slot[(i + 1) * ROWS : (i + 2) * ROWS]
-            first, second = chosen(dot(trace_s[...], stack3(mix)), face_send[:, cols])
-            first, second = turned(first, second, turn_send[:, cols])
-            rows = []
-            for at in range(2):
-                p = TILES[2 * half + at]
-                lanes = slice(at * 128, (at + 1) * 128)
-                send_buf[2 * p], send_buf[2 * p + 1] = packed(first[:, lanes], second[:, lanes])
-                rows += [2 * p, 2 * p + 1]
-            start(copy, [k for k in FAR_FIRST if k in rows])
-        meanwhile(j_all, j_two, traces(j_all), done)
-        arrive(copy)
-        parity = lax.rem(s, 2)
-        tiles = [unpacked(recv_buf[parity, 2 * p], recv_buf[parity, 2 * p + 1]) for p in TILES]
-        r0 = jnp.concatenate([t[0] for t in tiles], axis=1)
-        r1 = jnp.concatenate([t[1] for t in tiles], axis=1)
-        complete(r0, r1, done)
-        finish_sends(copy)
+        finish(s)
+        advance(s + 1)
         return carry
 
-    lax.fori_loop(1, SUBSTEPS, step, 0)
+    advance(1)
+    lax.fori_loop(1, SUBSTEPS - 1, step, 0)
+    finish(SUBSTEPS - 1, last=True)
     for q in range(QUANT):
         out[q] = u_s[q, 0:BASIS]
 
@@ -632,6 +699,10 @@
                 pltpu.VMEM((ROWS, 768), BF16),
                 pltpu.VMEM((6 * ROWS, 256), BF16),
                 pltpu.VMEM((2, ROWS, ELEMS), F32),
+                pltpu.VMEM((2, ROWS, ELEMS), F32),
+                pltpu.VMEM((4 * NROWS, 512), BF16),
+                pltpu.VMEM((16, SLOTS), F32),
+                pltpu.VMEM((8, SLOTS), F32),
                 pltpu.VMEM((2 * ELEMS, SLOTS), BF16),
                 pltpu.VMEM((2 * ELEMS, FACES), BF16),
                 pltpu.VMEM((SLOTS, ELEMS), BF16),

time: 33.2 us -> 32.1 us (0.967)
  Pallas kernels: 32 us -> 31.2 us
    pallas_call x1, Pallas kernels: 32 us -> 31.2 us  [call(): pl.pallas_call(lambda *refs: kernel(n_dev, *refs), out_shape=pltpu.VMEM((...]
where the time goes in v5:
time: 32.1 us; the launch traced here: 32 us
  Pallas kernels  31.2 us (97%)
  local copies, waits for them, and re-layouts  0.72 us (2%)
    pallas_call x1, Pallas kernels, call(): pl.pallas_call(lambda *refs: kernel(n_dev, *refs), out_shape=pltpu.VMEM((...  31.2 us
    pallas_call x1, local copies, waits for them, and re-layouts, call(): pl.pallas_call(lambda *refs: kernel(n_dev, *refs), out_shape=pltpu.VMEM((...  0.72 us

profile of v5, /device:TPU:25, one launch (start us, length us, event | category | flops | bytes accessed | tf_op | source)
XLA Modules:
  0.0 32.0 jit_solution(12874704156704582458)
XLA Ops:
  0.0 31.2 %shard_map.136 = f32[4,35,256]{2,1,0:T(8,128)S(1)} custom-call(f32[35,4,256]{2,1,0:T(4,128)} %bitcast.6, s32[1,256]{1,0:T(1,128)} %bitcast.9, s32[4,256]{1,0:T(4,128)} %refs_2_.1, s32[4,256]{1,0:T(4,128)} %refs_3_.1, s32[8,64]{1,0:T(8,128)} %refs_4_.1, s32[8,64]{1,0:T(8,128)} %refs_5_.1, f32[3,3,256]{2,1,0:T(4,128)} %refs_6_.1, f32[3,4,256]{2,1,0:T(4,128)} %bitcast.8, ...), custom_call_target="tpu_custom_call" | custom-call | tf_op jit(solution)/shard_map/pallas_call | solution.py:666
  31.2 0.7 %copy.15 = f32[4,35,256]{2,0,1:T(4,128)} copy(f32[4,35,256]{2,1,0:T(8,128)S(1)} %shard_map.136) | data formatting | bytes 286720 | tf_op jit(solution)/shard_map/pallas_call | solution.py:666

commit v6 on v5

--- a/solution.py
+++ b/solution.py
@@ -55,6 +55,11 @@
 def halves(x):
     hi = x.astype(BF16).astype(F32)
     return hi, x - hi
+
+
+def short_halves(x):
+    hi = x.astype(BF16)
+    return hi, (x - hi.astype(F32)).astype(BF16)
 
 
 def stack3(x):
@@ -316,10 +321,7 @@
         p_s[1] = twice(dot(second_s[...], stack3(u_s[0])))
 
     def two_parts(rows):
-        parts = [halves(x) for x in rows]
-        his = jnp.concatenate([p[0] for p in parts], axis=0)
-        los = jnp.concatenate([p[1] for p in parts], axis=0)
-        return jnp.concatenate([his, los], axis=1).astype(BF16)
+        return jnp.concatenate(short_halves(jnp.concatenate(rows, axis=0)), axis=1)
 
     def chosen(parts, faces):
         first, second = parts[0:8], parts[8:16]
@@ -438,8 +440,8 @@
 
     def stack4(flux):
         flux = jnp.concatenate([jnp.concatenate(rows, axis=0) for rows in flux], axis=1)
-        hi, lo = halves(flux)
-        return jnp.concatenate([hi, lo, hi, lo], axis=0).astype(BF16)
+        hi, lo = short_halves(flux)
+        return jnp.concatenate([hi, lo, hi, lo], axis=0)
 
     def placed(r0, r1, cols):
         r0h, r0l = halves(r0)
@@ -454,9 +456,9 @@
         return both[0:64] + both[64:128]
 
     def next_terms(flux, slopes, done):
-        hi, lo = halves(jnp.concatenate([x for rows in slopes for x in rows], axis=0))
-        pad = jnp.zeros((64, ELEMS), F32)
-        slopes = jnp.concatenate([hi, pad, lo, pad, hi, pad], axis=0).astype(BF16)
+        hi, lo = short_halves(jnp.concatenate([x for rows in slopes for x in rows], axis=0))
+        pad = jnp.zeros((64, ELEMS), BF16)
+        slopes = jnp.concatenate([hi, pad, lo, pad, hi, pad], axis=0)
         change_1 = bulk_v[...] * dot(flux1_s[...], slopes)
         change_2 = twice(dot(flux2_s[...], flux[:, 0:ELEMS]))
         p_s[0] = jnp.where(done, p_s[0] + change_1, p_s[0])

time: 32.1 us -> 32.1 us (level)
  no operation moved by 1% of the time
where the time goes in v6:
time: 32.1 us; the launch traced here: 32 us
  Pallas kernels  31.2 us (97%)
  local copies, waits for them, and re-layouts  0.72 us (2%)
    pallas_call x1, Pallas kernels, call(): pl.pallas_call(lambda *refs: kernel(n_dev, *refs), out_shape=pltpu.VMEM((...  31.2 us
    pallas_call x1, local copies, waits for them, and re-layouts, call(): pl.pallas_call(lambda *refs: kernel(n_dev, *refs), out_shape=pltpu.VMEM((...  0.72 us

profile of v6, /device:TPU:25, one launch (start us, length us, event | category | flops | bytes accessed | tf_op | source)
XLA Modules:
  0.0 32.0 jit_solution(11588975470145427880)
XLA Ops:
  0.0 31.2 %shard_map.136 = f32[4,35,256]{2,1,0:T(8,128)S(1)} custom-call(f32[35,4,256]{2,1,0:T(4,128)} %bitcast.6, s32[1,256]{1,0:T(1,128)} %bitcast.9, s32[4,256]{1,0:T(4,128)} %refs_2_.1, s32[4,256]{1,0:T(4,128)} %refs_3_.1, s32[8,64]{1,0:T(8,128)} %refs_4_.1, s32[8,64]{1,0:T(8,128)} %refs_5_.1, f32[3,3,256]{2,1,0:T(4,128)} %refs_6_.1, f32[3,4,256]{2,1,0:T(4,128)} %bitcast.8, ...), custom_call_target="tpu_custom_call" | custom-call | tf_op jit(solution)/shard_map/pallas_call | solution.py:668
  31.2 0.7 %copy.15 = f32[4,35,256]{2,0,1:T(4,128)} copy(f32[4,35,256]{2,1,0:T(8,128)S(1)} %shard_map.136) | data formatting | bytes 286720 | tf_op jit(solution)/shard_map/pallas_call | solution.py:668
